TPU v7x, 512 devices: a whole 4x8x8 slice. The times are simulated.
512 devices in a mesh: seq: 64 (over x, z, core), chan: 8 (over y).
Axes of the slice: x: 4, y: 8, z: 8, core: 2. Of those that a mesh axis runs over, the one named last changes fastest.
Arguments:
- projections: bfloat16 [3, 256, 32768], P(None, 'chan', 'seq'), may hold values from -6 to 6
- short_weight: float32 [3, 256, 3], P(None, 'chan'), may hold values from -3.5 to 3.5
- long_filter: bfloat16 [256, 32768], P('chan', 'seq'), may hold values from -0.03125 to 0.03125
- skip_gain: float32 [256], P('chan'), may hold values from 0.5 to 1.5
Outputs:
- gated: bfloat16 [256, 32768], P('chan', 'seq')
All inputs are finite; a program needn't handle non-finite values.
Results may differ from a plain program's by a relative error of at most 0.011.
Values may be sent and summed in bfloat16 or wider, within the bound.
A program may use at most 64 MiB of HBM per device.

v0:
```python
import math

import jax
import jax.numpy as jnp
from jax import lax
from jax.sharding import PartitionSpec as P

precise = lax.Precision.HIGHEST


def from_behind(x, axis, by):
    count = lax.axis_size(axis)
    pairs = [(i, i + by) for i in range(count) if 0 <= i + by < count]
    return lax.ppermute(x, axis, pairs)


def complex_product(left_re, left_im, right_re, right_im):
    return (left_re * right_re - left_im * right_im, left_re * right_im + left_im * right_re)


def phases(count_out, count_in, sign, length):
    rows = jnp.arange(count_out, dtype=jnp.int32)[:, None]
    cols = jnp.arange(count_in, dtype=jnp.int32)[None, :]
    angle = (rows * cols % length).astype(jnp.float32) * (2.0 * math.pi / length)
    return (jnp.cos(angle), sign * jnp.sin(angle))


def split_sizes(length):
    second = 128
    return (length // second, second)


def local_forward(real_part, imag_part):
    length = real_part.shape[-1]
    first, second = split_sizes(length)
    shape = real_part.shape[:-1] + (first, second)
    part_re = real_part.reshape(shape)
    part_im = imag_part.reshape(shape)
    mat_re, mat_im = phases(first, first, -1.0, first)
    step_re = jnp.einsum("kb,...bq->...kq", mat_re, part_re, precision=precise) - jnp.einsum(
        "kb,...bq->...kq", mat_im, part_im, precision=precise
    )
    step_im = jnp.einsum("kb,...bq->...kq", mat_re, part_im, precision=precise) + jnp.einsum(
        "kb,...bq->...kq", mat_im, part_re, precision=precise
    )
    turn_re, turn_im = phases(first, second, -1.0, length)
    step_re, step_im = complex_product(step_re, step_im, turn_re, turn_im)
    last_re, last_im = phases(second, second, -1.0, second)
    out_re = jnp.matmul(step_re, last_re, precision=precise) - jnp.matmul(
        step_im, last_im, precision=precise
    )
    out_im = jnp.matmul(step_re, last_im, precision=precise) + jnp.matmul(
        step_im, last_re, precision=precise
    )
    return (out_re, out_im)


def local_inverse(real_part, imag_part):
    first, second = (real_part.shape[-2], real_part.shape[-1])
    length = first * second
    last_re, last_im = phases(second, second, 1.0, second)
    step_re = jnp.matmul(real_part, last_re, precision=precise) - jnp.matmul(
        imag_part, last_im, precision=precise
    )
    step_im = jnp.matmul(real_part, last_im, precision=precise) + jnp.matmul(
        imag_part, last_re, precision=precise
    )
    turn_re, turn_im = phases(first, second, 1.0, length)
    step_re, step_im = complex_product(step_re, step_im, turn_re, turn_im)
    mat_re, mat_im = phases(first, first, 1.0, first)
    out_re = jnp.einsum("bk,...kq->...bq", mat_re, step_re, precision=precise) - jnp.einsum(
        "bk,...kq->...bq", mat_im, step_im, precision=precise
    )
    out_im = jnp.einsum("bk,...kq->...bq", mat_re, step_im, precision=precise) + jnp.einsum(
        "bk,...kq->...bq", mat_im, step_re, precision=precise
    )
    shape = real_part.shape[:-2] + (length,)
    return (out_re.reshape(shape) / length, out_im.reshape(shape) / length)


def shards(projections, short_weight, long_filter, skip_gain):
    tokens = projections.shape[2]
    blocks = lax.axis_size("seq")
    groups = lax.axis_size("chan")
    spread = 2 * blocks
    total = spread * tokens
    rim = from_behind(projections[:, :, tokens - 2 :], "seq", 1)
    extended = jnp.concatenate([rim, projections], axis=2).astype(jnp.float32)
    conv = short_weight[:, :, 0:1] * extended[:, :, :tokens]
    conv = conv + short_weight[:, :, 1:2] * extended[:, :, 1 : tokens + 1]
    conv = conv + short_weight[:, :, 2:3] * extended[:, :, 2:]
    conv = conv.astype(jnp.bfloat16)
    query = conv[0].astype(jnp.float32)
    mixed_in = (conv[1].astype(jnp.float32) * conv[2].astype(jnp.float32)).astype(jnp.bfloat16)
    paired = jnp.stack([mixed_in, long_filter])[:, None]
    seq_pos = lax.axis_index("seq")
    chan_pos = lax.axis_index("chan")
    columns = lax.all_to_all(
        lax.all_to_all(paired, "seq", split_axis=3, concat_axis=1, tiled=True),
        "chan",
        split_axis=3,
        concat_axis=2,
        tiled=True,
    )
    width = tokens // (blocks * groups)
    base = seq_pos * (tokens // blocks) + chan_pos * width
    slab = columns.shape[2]
    flat = columns.reshape(2, blocks, slab * width).astype(jnp.float32)
    first_re, first_im = phases(spread, blocks, -1.0, spread)
    spec_re = jnp.einsum("ca,saw->scw", first_re, flat, precision=precise)
    spec_im = jnp.einsum("ca,saw->scw", first_im, flat, precision=precise)
    position = jnp.arange(slab * width, dtype=jnp.int32) % width + base
    classes = jnp.arange(spread, dtype=jnp.int32)[:, None]
    angle = (classes * position[None, :] % total).astype(jnp.float32) * (2.0 * math.pi / total)
    twist_re = jnp.cos(angle)
    twist_im = -jnp.sin(angle)
    spec_re, spec_im = complex_product(spec_re, spec_im, twist_re, twist_im)
    spectra = jnp.stack([spec_re, spec_im], 1).reshape(2, 2, spread, slab, 1, 1, width)
    rowwise = lax.all_to_all(
        lax.all_to_all(spectra, "seq", split_axis=2, concat_axis=4, tiled=True),
        "chan",
        split_axis=3,
        concat_axis=5,
        tiled=True,
    )
    rowwise = rowwise.reshape(2, 2, 2, slab // groups, tokens)
    freq_re, freq_im = local_forward(rowwise[:, 0], rowwise[:, 1])
    prod_re, prod_im = complex_product(freq_re[0], freq_im[0], freq_re[1], freq_im[1])
    back_re, back_im = local_inverse(prod_re, prod_im)
    returned = jnp.stack([back_re, back_im])
    gathered = lax.all_to_all(
        lax.all_to_all(
            returned.astype(jnp.bfloat16), "seq", split_axis=3, concat_axis=1, tiled=True
        ),
        "chan",
        split_axis=3,
        concat_axis=2,
        tiled=True,
    ).astype(returned.dtype)
    mix_re = gathered[0].reshape(spread, slab * width)
    mix_im = gathered[1].reshape(spread, slab * width)
    mix_re, mix_im = complex_product(mix_re, mix_im, twist_re, -twist_im)
    last_re, last_im = phases(blocks, spread, 1.0, spread)
    signal = (
        jnp.matmul(last_re, mix_re, precision=precise)
        - jnp.matmul(last_im, mix_im, precision=precise)
    ) / spread
    signal = signal.reshape(blocks, slab, 1, 1, width)
    restored = lax.all_to_all(
        lax.all_to_all(signal, "seq", split_axis=0, concat_axis=2, tiled=True),
        "chan",
        split_axis=1,
        concat_axis=3,
        tiled=True,
    )
    restored = restored.reshape(1, slab // groups, tokens)
    long_out = restored[0]
    gated = query * (long_out + skip_gain[:, None] * mixed_in.astype(jnp.float32))
    return gated.astype(jnp.bfloat16)


def solution(mesh):
    in_specs = (P(None, "chan", "seq"), P(None, "chan", None), P("chan", "seq"), P("chan"))
    out_specs = P("chan", "seq")
    return jax.shard_map(shards, mesh=mesh, in_specs=in_specs, out_specs=out_specs, check_vma=False)
```

profile of v0, /device:TPU:1, one launch (start us, length us, event | category | flops | bytes accessed | tf_op | source)
XLA Modules:
  0.0 172.1 jit_solution(15927112386941106626)
XLA Ops:
  0.0 0.8 slice.57
  0.8 5.4 %collective-permute-start = (bf16[3,32,2]{2,1,0:T(8,128)(2,1)S(1)}, bf16[3,32,2]{2,1,0:T(8,128)(2,1)S(1)}, u32[]{:S(2)}, u32[]{:S(2)}) collective-permute-start(bf16[3,32,2]{2,1,0:T(8,128)(2,1)S(1)} %slice.57), channel_id=1, source_target_pairs={{0,8},{8,16},{16,24},{24,32},{32,40},{40,48},{48,56},{56,64},{64,7... | collective-permute-start | bytes 1160 | tf_op jit(solution)/shard_map/ppermute | solution.py:14
  6.2 0.8 fusion.217
  7.0 0.9 copy.137
  7.9 1.7 %collective-permute-done = bf16[3,32,2]{2,1,0:T(8,128)(2,1)S(1)} collective-permute-done((bf16[3,32,2]{2,1,0:T(8,128)(2,1)S(1)}, bf16[3,32,2]{2,1,0:T(8,128)(2,1)S(1)}, u32[]{:S(2)}, u32[]{:S(2)}) %collective-permute-start) | collective-permute-done | bytes 416 | tf_op jit(solution)/shard_map/ppermute | solution.py:14
  9.6 1.0 pad_maximum_fusion.1
  11.6 0.8 reshape.205
  12.4 12.3 %all-to-all-start = ((bf16[64,2,256]{2,1,0:T(2,128)(2,1)}), bf16[64,2,256]{2,1,0:T(2,128)(2,1)S(1)}, u32[]{:S(2)}, u32[]{:S(2)}) async-start(bf16[64,2,256]{2,1,0:T(2,128)(2,1)} %reshape.205), calls=%async_computation | async-start | bytes 131072 | tf_op jit(solution)/shard_map/all_to_all | solution.py:99
  24.8 9.8 %all-to-all-done = bf16[64,2,256]{2,1,0:T(2,128)(2,1)S(1)} async-done(((bf16[64,2,256]{2,1,0:T(2,128)(2,1)}), bf16[64,2,256]{2,1,0:T(2,128)(2,1)S(1)}, u32[]{:S(2)}, u32[]{:S(2)}) %all-to-all-start) | async-done | bytes 65568 | tf_op jit(solution)/shard_map/all_to_all | solution.py:99
  35.0 0.8 reshape.207
  35.8 6.8 %all-to-all-start.1 = ((bf16[8,2,2048]{2,1,0:T(2,128)(2,1)}), bf16[8,2,2048]{2,1,0:T(2,128)(2,1)S(1)}, u32[]{:S(2)}, u32[]{:S(2)}) async-start(bf16[8,2,2048]{2,1,0:T(2,128)(2,1)} %reshape.207), calls=%async_computation.1 | async-start | bytes 131072 | tf_op jit(solution)/shard_map/all_to_all | solution.py:98
  42.7 7.2 %all-to-all-done.1 = bf16[8,2,2048]{2,1,0:T(2,128)(2,1)S(1)} async-done(((bf16[8,2,2048]{2,1,0:T(2,128)(2,1)}), bf16[8,2,2048]{2,1,0:T(2,128)(2,1)S(1)}, u32[]{:S(2)}, u32[]{:S(2)}) %all-to-all-start.1) | async-done | bytes 65568 | tf_op jit(solution)/shard_map/all_to_all | solution.py:98
  51.1 22.6 %all_to_all.126 = f32[2,2,128,256,1,1,1]{3,0,1,6,5,4,2:T(2,128)S(1)} all-to-all(f32[2,2,128,256,1,1,1]{3,0,1,6,5,4,2:T(2,128)S(1)} %copy.144), channel_id=1, replica_groups=mesh['seq'=64,'chan'=8] {'seq'}, dimensions={2} | all-to-all | bytes 1048576 | tf_op jit(solution)/shard_map/all_to_all | solution.py:120
  74.0 0.9 copy.146
  74.9 1.9 %reshape.209 = f32[8,1,16384]{2,1,0:T(1,128)} reshape(f32[256,2,2,1,1,2,64]{6,5,4,3,2,1,0:T(2,128)S(1)} %bitcast.201) | data formatting | bytes 1048576
  76.8 3.7 %all-to-all-start.3 = ((f32[8,1,16384]{2,1,0:T(1,128)}), f32[8,1,16384]{2,1,0:T(1,128)S(1)}, u32[]{:S(2)}, u32[]{:S(2)}) async-start(f32[8,1,16384]{2,1,0:T(1,128)} %reshape.209), calls=%async_computation.3 | async-start | bytes 1048576 | tf_op jit(solution)/shard_map/all_to_all | solution.py:119
  80.6 16.3 %all-to-all-done.3 = f32[8,1,16384]{2,1,0:T(1,128)S(1)} async-done(((f32[8,1,16384]{2,1,0:T(1,128)}), f32[8,1,16384]{2,1,0:T(1,128)S(1)}, u32[]{:S(2)}, u32[]{:S(2)}) %all-to-all-start.3) | async-done | bytes 524320 | tf_op jit(solution)/shard_map/all_to_all | solution.py:119
  97.4 1.9 %reduce = f32[8,16384]{1,0:T(8,128)S(1)} reduce(f32[8,1,16384]{2,1,0:T(1,128)S(1)} %all-to-all-done.3, f32[]{:T(128)} %broadcast.472), dimensions={1}, to_apply=%all_to_all.103.reduce_sub_computation | reduce | bytes 1048580 | tf_op jit(solution)/shard_map/all_to_all | solution.py:119
  99.3 0.8 reshape.210
  100.3 0.7 copy.148
  101.0 1.1 fusion.215
  102.1 1.5 copy.178
  105.8 0.7 multiply_add_fusion
  107.1 0.6 fusion.18
  107.8 0.6 convolution_subtract_fusion
  114.1 17.2 %all_to_all.127 = bf16[64,2,512]{2,1,0:T(2,128)(2,1)S(1)} all-to-all(bf16[64,2,512]{2,1,0:T(2,128)(2,1)S(1)} %reshape.211), channel_id=1, replica_groups=mesh['seq'=64,'chan'=8] {'seq'}, dimensions={0} | all-to-all | bytes 262144 | tf_op jit(solution)/shard_map/all_to_all | solution.py:132
  132.1 10.8 %all_to_all.128 = bf16[2,128,32,8]{1,2,0,3:T(8,128)(2,1)S(1)} all-to-all(bf16[2,128,32,8]{1,2,0,3:T(8,128)(2,1)S(1)} %copy.162), channel_id=1, replica_groups=mesh['seq'=64,'chan'=8] {'chan'}, dimensions={3} | all-to-all | bytes 262144 | tf_op jit(solution)/shard_map/all_to_all | solution.py:131
  143.8 15.6 %all_to_all.129 = f32[64,256,1,1,1]{1,4,3,2,0:T(1,128)S(1)} all-to-all(f32[64,256,1,1,1]{1,4,3,2,0:T(1,128)S(1)} %copy.164), channel_id=1, replica_groups=mesh['seq'=64,'chan'=8] {'seq'}, dimensions={0} | all-to-all | bytes 131072 | tf_op jit(solution)/shard_map/all_to_all | solution.py:150
  159.5 1.0 reduce.1
  160.6 9.5 %all_to_all.130 = f32[8,1,2048]{2,1,0:T(1,128)S(1)} all-to-all(f32[8,1,2048]{2,1,0:T(1,128)S(1)} %reshape.213), channel_id=1, replica_groups=mesh['seq'=64,'chan'=8] {'chan'}, dimensions={0} | all-to-all | bytes 131072 | tf_op jit(solution)/shard_map/all_to_all | solution.py:149
  170.1 0.8 reduce.2
  171.4 0.7 copy.167
  (61 shorter events, 14.3 us)
Async XLA Ops:
  0.8 8.8 %collective-permute-start = (bf16[3,32,2]{2,1,0:T(8,128)(2,1)S(1)}, bf16[3,32,2]{2,1,0:T(8,128)(2,1)S(1)}, u32[]{:S(2)}, u32[]{:S(2)}) collective-permute-start(bf16[3,32,2]{2,1,0:T(8,128)(2,1)S(1)} %slice.57), channel_id=1, source_target_pairs={{0,8},{8,16},{16,24},{24,32},{32,40},{40,48},{48,56},{56,64},{64,7... | collective-permute-start | bytes 1160 | tf_op jit(solution)/shard_map/ppermute | solution.py:14
  12.4 22.1 %all-to-all-start = ((bf16[64,2,256]{2,1,0:T(2,128)(2,1)}), bf16[64,2,256]{2,1,0:T(2,128)(2,1)S(1)}, u32[]{:S(2)}, u32[]{:S(2)}) async-start(bf16[64,2,256]{2,1,0:T(2,128)(2,1)} %reshape.205), calls=%async_computation | async-start | bytes 131072 | tf_op jit(solution)/shard_map/all_to_all | solution.py:99
  35.8 14.1 %all-to-all-start.1 = ((bf16[8,2,2048]{2,1,0:T(2,128)(2,1)}), bf16[8,2,2048]{2,1,0:T(2,128)(2,1)S(1)}, u32[]{:S(2)}, u32[]{:S(2)}) async-start(bf16[8,2,2048]{2,1,0:T(2,128)(2,1)} %reshape.207), calls=%async_computation.1 | async-start | bytes 131072 | tf_op jit(solution)/shard_map/all_to_all | solution.py:98
  76.8 20.1 %all-to-all-start.3 = ((f32[8,1,16384]{2,1,0:T(1,128)}), f32[8,1,16384]{2,1,0:T(1,128)S(1)}, u32[]{:S(2)}, u32[]{:S(2)}) async-start(f32[8,1,16384]{2,1,0:T(1,128)} %reshape.209), calls=%async_computation.3 | async-start | bytes 1048576 | tf_op jit(solution)/shard_map/all_to_all | solution.py:119
  132.1 39.2 %copy-start = (f32[32]{0:T(128)S(1)}, f32[32]{0:T(128)}, u32[]{:S(2)}) copy-start(f32[32]{0:T(128)} %param.7) | copy-start | bytes 388
where the time goes:
time: 173 us; the launch traced here: 172 us
  blocking collectives  75.7 us (44%)
  waiting for transfers between devices  35 us (20%)
  starting transfers between devices  28.2 us (16%)
  local copies, waits for them, and re-layouts  16.9 us (10%)
  matrix products  10.3 us (6%)
  other arithmetic  5.5 us (3%)
    all_to_all x1, blocking collectives, shards(): lax.all_to_all(spectra, 'seq', split_axis=2, concat_axis=4, tiled=True)  22.6 us
    all_to_all x1, blocking collectives, shards(): lax.all_to_all(returned.astype(jnp.bfloat16), 'seq', split_axis=3, concat...  17.2 us
    all_to_all x1, waiting for transfers between devices, shards(): lax.all_to_all(lax.all_to_all(spectra, 'seq', split_axis=2, concat_axis=4...  16.3 us
    all_to_all x1, blocking collectives, shards(): lax.all_to_all(signal, 'seq', split_axis=0, concat_axis=2, tiled=True)  15.6 us
    all_to_all x1, starting transfers between devices, shards(): lax.all_to_all(paired, 'seq', split_axis=3, concat_axis=1, tiled=True)  12.3 us
    all_to_all x1, blocking collectives, shards(): lax.all_to_all(lax.all_to_all(returned.astype(jnp.bfloat16), 'seq', split...  10.8 us
    all_to_all x1, waiting for transfers between devices, shards(): lax.all_to_all(paired, 'seq', split_axis=3, concat_axis=1, tiled=True)  9.78 us
    all_to_all x1, blocking collectives, shards(): lax.all_to_all(lax.all_to_all(signal, 'seq', split_axis=0, concat_axis=2,...  9.51 us
  transfers between devices with their start and end apart: 4, of which 4 were waited for; matrix products, arithmetic and copies ran while one was open for 1% of the time, Pallas kernels for 0%

commit v1 on v0

v1 whole, which is shorter than its diff:
```python
import functools

import jax
import jax.numpy as jnp
import numpy as np
from jax import lax
from jax.experimental import pallas as pl
from jax.experimental.pallas import tpu as pltpu
from jax.sharding import PartitionSpec as P

MESH = pl.DeviceIdType.MESH
LANES = 128
f32 = jnp.float32
bf16 = jnp.bfloat16


def tables(blocks, pieces):
    rows = blocks * pieces
    n = rows * LANES
    order = (np.arange(blocks)[None, :] * pieces + np.arange(pieces)[:, None]).reshape(-1)
    k1 = np.arange(rows) + 0.25
    first = np.exp(-2j * np.pi * np.outer(k1, order) / rows)
    turn = np.exp(-2j * np.pi * np.outer(k1, np.arange(LANES)) / n)
    second = np.exp(-2j * np.pi * np.outer(np.arange(LANES), np.arange(LANES)) / LANES)
    back = np.conj(second)
    last = np.conj(first).T / n
    w1 = np.concatenate([first.real, first.imag], 0)
    w3 = np.block([[second.real, second.imag], [-second.imag, second.real]])
    w4 = np.block([[back.real, back.imag], [-back.imag, back.real]])
    w6 = np.concatenate([last.real, -last.imag], 1)
    tw = np.stack([turn.real, turn.imag])
    return tuple(x.astype(np.float32) for x in (w1, w3, w4, w6, tw))


def dot(a, b):
    return jnp.dot(a, b, preferred_element_type=f32)


def kernel(
    blocks, proj, weight, filt, gain, w1, w3, w4, w6, tw, out,
    proj_v, filt_v, weight_v, gain_s, w1_v, w3_v, w4_v, w6_v, tw_v,
    spread, msg, inbox, opened, result, back, out_v,
    load_sem, const_sem, send_sem, recv_sem, send2_sem, recv2_sem,
):
    chips = blocks // 2
    chans = proj.shape[1]
    pieces = proj.shape[2] // LANES
    me = lax.axis_index("seq")
    chip = me // 2
    core = lax.rem(me, 2)
    first_core = core == 0
    loads = [
        pltpu.make_async_copy(proj, proj_v, load_sem.at[0]),
        pltpu.make_async_copy(filt, filt_v, load_sem.at[1]),
    ]
    for load in loads:
        load.start()
    consts = [
        pltpu.make_async_copy(src, dst, const_sem.at[i])
        for i, (src, dst) in enumerate(
            [(w1, w1_v), (w3, w3_v), (w4, w4_v), (w6, w6_v), (tw, tw_v), (weight, weight_v), (gain, gain_s)]
        )
    ]

    barrier = pltpu.get_barrier_semaphore()

    @pl.when(first_core)
    def _():
        def greet(i, carry):
            pl.semaphore_signal(
                barrier, inc=1, device_id={"seq": lax.rem(me + i, blocks)}, device_id_type=MESH
            )
            return carry

        lax.fori_loop(1, blocks, greet, 0)

    @pl.when(core == 1)
    def _():
        def greet(i, carry):
            pl.semaphore_signal(
                barrier, inc=1, device_id={"seq": 2 * lax.rem(chip + i, chips)}, device_id_type=MESH
            )
            return carry

        lax.fori_loop(0, chips, greet, 0)

    @pl.when(first_core)
    def _():
        for const in consts:
            const.start()

    for load in loads:
        load.wait()
    for j in range(4):
        for r in range(pieces):
            cols = slice(LANES * r, LANES * (r + 1))
            piece = proj_v[j, :, cols] if j < 3 else filt_v[:, cols]
            spread[pl.ds(j * pieces + r, chans, stride=4 * pieces), :] = piece.astype(f32)
    msg[...] = spread[...].reshape(chans, 4 * pieces, LANES).astype(bf16)

    @pl.when(first_core)
    def _():
        pl.semaphore_wait(barrier, blocks - 1)

    @pl.when(core == 1)
    def _():
        pl.semaphore_wait(barrier, chips)

    def send(i, carry):
        p = lax.rem(chip + i, chips)
        pltpu.make_async_remote_copy(
            src_ref=msg.at[p],
            dst_ref=inbox.at[me],
            send_sem=send_sem,
            recv_sem=recv_sem,
            device_id={"seq": 2 * p},
            device_id_type=MESH,
        ).start()
        return carry

    @pl.when(core == 1)
    def _():
        send(0, 0)

    lax.fori_loop(1, chips, send, 0)

    @pl.when(first_core)
    def _():
        inbox[me] = msg[chip]
        for const in consts:
            const.wait()
        others = inbox.at[pl.ds(0, blocks - 1)]
        pltpu.make_async_copy(others, others, recv_sem).wait()
        opened[...] = inbox[...].astype(f32).reshape(blocks * 4 * pieces, LANES)
        part = [
            [opened[pl.ds(j * pieces + r, blocks, stride=4 * pieces), :] for r in range(pieces)]
            for j in range(4)
        ]
        lane = lax.broadcasted_iota(jnp.int32, (blocks, LANES), 1)
        row = lax.broadcasted_iota(jnp.int32, (blocks, LANES), 0)
        chan_lane = lax.broadcasted_iota(jnp.int32, weight_v.shape[1:], 1)
        conv = []
        for j in range(3):
            taps = jnp.sum(jnp.where(chan_lane == chip, weight_v[j], 0.0), axis=1, keepdims=True)
            before = jnp.where(row == 0, 0.0, pltpu.roll(part[j][pieces - 1], 1, 0))
            done = []
            for r in range(pieces):
                now = part[j][r]
                one = pltpu.roll(jnp.where(lane >= LANES - 1, before, now), 1, 1)
                two = pltpu.roll(jnp.where(lane >= LANES - 2, before, now), 2, 1)
                total = taps[0:1, :] * two
                total = total + taps[1:2, :] * one
                total = total + taps[2:3, :] * now
                done.append(total.astype(bf16).astype(f32))
                before = now
            conv.append(jnp.concatenate(done, 0))
        query, key, value = conv
        mixed = (key * value).astype(bf16)
        taps = jnp.concatenate(part[3], 0).astype(bf16)
        rows = blocks * pieces
        both = jnp.concatenate([mixed, taps], 1)
        step = dot(w1_v[...].astype(bf16), both)
        tr, ti = tw_v[0], tw_v[1]
        turned = []
        for half in (slice(0, LANES), slice(LANES, 2 * LANES)):
            re, im = step[:rows, half], step[rows:, half]
            turned.append(jnp.concatenate([re * tr - im * ti, re * ti + im * tr], 1).astype(bf16))
        spec = dot(jnp.concatenate(turned, 0), w3_v[...].astype(bf16))
        xr, xi = spec[:rows, :LANES], spec[:rows, LANES:]
        hr, hi = spec[rows:, :LANES], spec[rows:, LANES:]
        prod = jnp.concatenate([xr * hr - xi * hi, xr * hi + xi * hr], 1).astype(bf16)
        inv = dot(prod, w4_v[...].astype(bf16))
        re, im = inv[:, :LANES], inv[:, LANES:]
        untwist = jnp.concatenate([re * tr + im * ti, im * tr - re * ti], 0).astype(bf16)
        long_out = dot(w6_v[...].astype(bf16), untwist)
        gated = query * (long_out + gain_s[chip] * mixed.astype(f32))
        for r in range(pieces):
            result[pl.ds(r, blocks, stride=pieces), :] = gated[r * blocks : (r + 1) * blocks]
        back[chip] = result[pl.ds(pl.multiple_of(me * pieces, pieces), pieces), :]

        def reply(i, carry):
            a = lax.rem(me + i, blocks)
            pltpu.make_async_remote_copy(
                src_ref=result.at[pl.ds(pl.multiple_of(a * pieces, pieces), pieces), :],
                dst_ref=back.at[chip],
                send_sem=send2_sem,
                recv_sem=recv2_sem,
                device_id={"seq": a},
                device_id_type=MESH,
            ).start()
            return carry

        lax.fori_loop(1, blocks, reply, 0)
        mine = back.at[pl.ds(0, chips - 1)]
        pltpu.make_async_copy(mine, mine, recv2_sem).wait()

    @pl.when(core == 1)
    def _():
        pltpu.make_async_copy(back, back, recv2_sem).wait()

    for r in range(pieces):
        out_v[:, LANES * r : LANES * (r + 1)] = back[:, r, :].astype(bf16)
    store = pltpu.make_async_copy(out_v, out, load_sem.at[2])
    store.start()

    @pl.when(first_core)
    def _():
        sent = msg.at[pl.ds(0, chips - 1)]
        pltpu.make_async_copy(sent, sent, send_sem).wait()
        sent = result.at[pl.ds(0, (blocks - 1) * pieces), :]
        pltpu.make_async_copy(sent, sent, send2_sem).wait()

    @pl.when(core == 1)
    def _():
        pltpu.make_async_copy(msg, msg, send_sem).wait()

    store.wait()


def shards(blocks, projections, short_weight, long_filter, skip_gain):
    _, chans, tokens = projections.shape
    pieces = tokens // LANES
    rows = blocks * pieces
    consts = [jnp.asarray(x) for x in tables(blocks, pieces)]
    weight = jnp.transpose(short_weight, (0, 2, 1))
    dma = pltpu.SemaphoreType.DMA
    scratch = [
        pltpu.VMEM(projections.shape, bf16),
        pltpu.VMEM(long_filter.shape, bf16),
        pltpu.VMEM(weight.shape, f32),
        pltpu.SMEM(skip_gain.shape, f32),
        *[pltpu.VMEM(x.shape, x.dtype) for x in consts],
        pltpu.VMEM((chans * 4 * pieces, LANES), f32),
        pltpu.VMEM((chans, 4 * pieces, LANES), bf16),
        pltpu.VMEM((blocks, 4 * pieces, LANES), bf16),
        pltpu.VMEM((blocks * 4 * pieces, LANES), f32),
        pltpu.VMEM((rows, LANES), f32),
        pltpu.VMEM((chans, pieces, LANES), f32),
        pltpu.VMEM((chans, tokens), bf16),
        dma((3,)), dma((7,)), dma, dma, dma, dma,
    ]
    return pl.pallas_call(
        functools.partial(kernel, blocks),
        out_shape=jax.ShapeDtypeStruct((chans, tokens), bf16),
        in_specs=[pl.BlockSpec(memory_space=pl.ANY)] * 9,
        out_specs=pl.BlockSpec(memory_space=pl.ANY),
        scratch_shapes=scratch,
        compiler_params=pltpu.CompilerParams(
            collective_id=0, has_side_effects=True, vmem_limit_bytes=56 * 1024 * 1024
        ),
        cost_estimate=pl.CostEstimate(flops=200_000_000, bytes_accessed=2_000_000, transcendentals=0),
        name="hyena",
    )(projections, weight, long_filter, skip_gain, *consts)


def solution(mesh):
    in_specs = (P(None, "chan", "seq"), P(None, "chan", None), P("chan", "seq"), P("chan"))
    out_specs = P("chan", "seq")
    body = functools.partial(shards, mesh.shape["seq"])
    return jax.shard_map(body, mesh=mesh, in_specs=in_specs, out_specs=out_specs, check_vma=False)
```

time: 173 us -> 31 us (0.18)
  blocking collectives: 75.7 us -> 0 us
  waiting for transfers between devices: 35 us -> 0 us
  Pallas kernels: 0 us -> 29.4 us
  starting transfers between devices: 28.2 us -> 0 us
  local copies, waits for them, and re-layouts: 16.9 us -> 1.38 us
  matrix products: 10.3 us -> 0 us
  other arithmetic: 5.5 us -> 0 us
    all_to_all x5 -> x0, blocking collectives: 75.7 us -> none  [the longest x1 22.6 us: shards(): lax.all_to_all(spectra, 'seq', split_axis=2, concat_axis=4, tiled=True)]
    all_to_all x3 -> x0, waiting for transfers between devices: 33.2 us -> none  [the longest x1 16.3 us: shards(): lax.all_to_all(lax.all_to_all(spectra, 'seq', split_axis=2, concat_axis=4...]
    pallas_call x0 -> x1, Pallas kernels: none -> 29.4 us  [shards(): pl.pallas_call(functools.partial(kernel, blocks), out_shape=jax.ShapeDtyp...]
    all_to_all x3 -> x0, starting transfers between devices: 22.8 us -> none  [the longest x1 12.3 us: shards(): lax.all_to_all(paired, 'seq', split_axis=3, concat_axis=1, tiled=True)]
    dot_general x20 -> x0, matrix products: 10.3 us -> none  [the longest x1 0.69 us: local_forward(): jnp.einsum('kb,...bq->...kq', mat_im, part_re, precision=precise)]
    ppermute x1 -> x0, starting transfers between devices: 5.38 us -> none  [from_behind(): return lax.ppermute(x, axis, pairs)]
    unnamed x15 -> x1, local copies, waits for them, and re-layouts: 6.46 us -> 1.38 us
    all_to_all x14 -> x0, local copies, waits for them, and re-layouts: 3.62 us -> none  [the longest x3 1.42 us: shards(): lax.all_to_all(lax.all_to_all(spectra, 'seq', split_axis=2, concat_axis=4...]
  transfers between devices with their start and end apart: 4 -> 0, of which waited for: 4 -> 0; matrix products, arithmetic and copies ran while one was open for 1% -> 0% of each run, Pallas kernels for 0% -> 0%
where the time goes in v1:
time: 31 us; the launch traced here: 30.8 us
  Pallas kernels  29.4 us (95%)
  local copies, waits for them, and re-layouts  1.38 us (4%)
    pallas_call x1, Pallas kernels, shards(): pl.pallas_call(functools.partial(kernel, blocks), out_shape=jax.ShapeDtyp...  29.4 us
    unnamed x1, local copies, waits for them, and re-layouts  1.38 us

profile of v1, /device:TPU:1, one launch (start us, length us, event | category | flops | bytes accessed | tf_op | source)
XLA Modules:
  0.0 30.8 jit_solution(6421559619008225016)
XLA Ops:
  0.0 29.4 %hyena.1 = bf16[32,512]{1,0:T(8,128)(2,1)} custom-call(bf16[3,32,512]{2,1,0:T(8,128)(2,1)} %proj.1, f32[3,3,32]{2,1,0:T(4,128)} %bitcast.1, bf16[32,512]{1,0:T(8,128)(2,1)} %filt.1, f32[32]{0:T(128)} %gain.1, f32[512,256]{1,0:T(8,128)} %constant.10.clone.w1, f32[256,256]{1,0:T(8,128)} %constant.11.clone.w3, f32[256,256]{1,0:T(8,128)} %constant.12.clone.w4, ...), custom_call_target="tpu_custom_call" | custom-call | flops 200000000 | bytes 2000000 | tf_op jit(solution)/shard_map/hyena/pallas_call | solution.py:242
  29.5 1.4 %copy.11 = bf16[32,512]{1,0:T(8,128)(2,1)} copy(bf16[32,512]{1,0:T(8,128)(2,1)} %hyena.1) | data formatting | bytes 65536

commit v2 on v1

--- a/solution.py
+++ b/solution.py
@@ -10,6 +10,7 @@
 
 MESH = pl.DeviceIdType.MESH
 LANES = 128
+GROUP = 8
 f32 = jnp.float32
 bf16 = jnp.bfloat16
 
@@ -42,13 +43,16 @@
     spread, msg, inbox, opened, result, back, out_v,
     load_sem, const_sem, send_sem, recv_sem, send2_sem, recv2_sem,
 ):
-    chips = blocks // 2
     chans = proj.shape[1]
     pieces = proj.shape[2] // LANES
     me = lax.axis_index("seq")
-    chip = me // 2
-    core = lax.rem(me, 2)
-    first_core = core == 0
+    group, place = me // (2 * GROUP), lax.rem(me, 2 * GROUP)
+    holder = place < GROUP
+    mine = group * GROUP + lax.rem(place, GROUP)
+
+    def home(ch):
+        return (ch // GROUP) * (2 * GROUP) + lax.rem(ch, GROUP)
+
     loads = [
         pltpu.make_async_copy(proj, proj_v, load_sem.at[0]),
         pltpu.make_async_copy(filt, filt_v, load_sem.at[1]),
@@ -64,7 +68,7 @@
 
     barrier = pltpu.get_barrier_semaphore()
 
-    @pl.when(first_core)
+    @pl.when(holder)
     def _():
         def greet(i, carry):
             pl.semaphore_signal(
@@ -73,19 +77,6 @@
             return carry
 
         lax.fori_loop(1, blocks, greet, 0)
-
-    @pl.when(core == 1)
-    def _():
-        def greet(i, carry):
-            pl.semaphore_signal(
-                barrier, inc=1, device_id={"seq": 2 * lax.rem(chip + i, chips)}, device_id_type=MESH
-            )
-            return carry
-
-        lax.fori_loop(0, chips, greet, 0)
-
-    @pl.when(first_core)
-    def _():
         for const in consts:
             const.start()
 
@@ -98,35 +89,35 @@
             spread[pl.ds(j * pieces + r, chans, stride=4 * pieces), :] = piece.astype(f32)
     msg[...] = spread[...].reshape(chans, 4 * pieces, LANES).astype(bf16)
 
-    @pl.when(first_core)
-    def _():
-        pl.semaphore_wait(barrier, blocks - 1)
-
-    @pl.when(core == 1)
-    def _():
-        pl.semaphore_wait(barrier, chips)
+    @pl.when(holder)
+    def _():
+        pl.semaphore_wait(barrier, chans - 1)
+
+    @pl.when(jnp.logical_not(holder))
+    def _():
+        pl.semaphore_wait(barrier, chans)
 
     def send(i, carry):
-        p = lax.rem(chip + i, chips)
+        ch = lax.rem(mine + i, chans)
         pltpu.make_async_remote_copy(
-            src_ref=msg.at[p],
+            src_ref=msg.at[ch],
             dst_ref=inbox.at[me],
             send_sem=send_sem,
             recv_sem=recv_sem,
-            device_id={"seq": 2 * p},
+            device_id={"seq": home(ch)},
             device_id_type=MESH,
         ).start()
         return carry
 
-    @pl.when(core == 1)
+    @pl.when(jnp.logical_not(holder))
     def _():
         send(0, 0)
 
-    lax.fori_loop(1, chips, send, 0)
-
-    @pl.when(first_core)
-    def _():
-        inbox[me] = msg[chip]
+    lax.fori_loop(1, chans, send, 0)
+
+    @pl.when(holder)
+    def _():
+        inbox[me] = msg[mine]
         for const in consts:
             const.wait()
         others = inbox.at[pl.ds(0, blocks - 1)]
@@ -141,7 +132,7 @@
         chan_lane = lax.broadcasted_iota(jnp.int32, weight_v.shape[1:], 1)
         conv = []
         for j in range(3):
-            taps = jnp.sum(jnp.where(chan_lane == chip, weight_v[j], 0.0), axis=1, keepdims=True)
+            taps = jnp.sum(jnp.where(chan_lane == mine, weight_v[j], 0.0), axis=1, keepdims=True)
             before = jnp.where(row == 0, 0.0, pltpu.roll(part[j][pieces - 1], 1, 0))
             done = []
             for r in range(pieces):
@@ -173,16 +164,16 @@
         re, im = inv[:, :LANES], inv[:, LANES:]
         untwist = jnp.concatenate([re * tr + im * ti, im * tr - re * ti], 0).astype(bf16)
         long_out = dot(w6_v[...].astype(bf16), untwist)
-        gated = query * (long_out + gain_s[chip] * mixed.astype(f32))
+        gated = query * (long_out + gain_s[mine] * mixed.astype(f32))
         for r in range(pieces):
             result[pl.ds(r, blocks, stride=pieces), :] = gated[r * blocks : (r + 1) * blocks]
-        back[chip] = result[pl.ds(pl.multiple_of(me * pieces, pieces), pieces), :]
+        back[mine] = result[pl.ds(pl.multiple_of(me * pieces, pieces), pieces), :]
 
         def reply(i, carry):
             a = lax.rem(me + i, blocks)
             pltpu.make_async_remote_copy(
                 src_ref=result.at[pl.ds(pl.multiple_of(a * pieces, pieces), pieces), :],
-                dst_ref=back.at[chip],
+                dst_ref=back.at[mine],
                 send_sem=send2_sem,
                 recv_sem=recv2_sem,
                 device_id={"seq": a},
@@ -191,10 +182,10 @@
             return carry
 
         lax.fori_loop(1, blocks, reply, 0)
-        mine = back.at[pl.ds(0, chips - 1)]
-        pltpu.make_async_copy(mine, mine, recv2_sem).wait()
-
-    @pl.when(core == 1)
+        others = back.at[pl.ds(0, chans - 1)]
+        pltpu.make_async_copy(others, others, recv2_sem).wait()
+
+    @pl.when(jnp.logical_not(holder))
     def _():
         pltpu.make_async_copy(back, back, recv2_sem).wait()
 
@@ -203,14 +194,14 @@
     store = pltpu.make_async_copy(out_v, out, load_sem.at[2])
     store.start()
 
-    @pl.when(first_core)
-    def _():
-        sent = msg.at[pl.ds(0, chips - 1)]
+    @pl.when(holder)
+    def _():
+        sent = msg.at[pl.ds(0, chans - 1)]
         pltpu.make_async_copy(sent, sent, send_sem).wait()
         sent = result.at[pl.ds(0, (blocks - 1) * pieces), :]
         pltpu.make_async_copy(sent, sent, send2_sem).wait()
 
-    @pl.when(core == 1)
+    @pl.when(jnp.logical_not(holder))
     def _():
         pltpu.make_async_copy(msg, msg, send_sem).wait()
 

time: 31 us -> 30.9 us (level)
  no operation moved by 1% of the time
where the time goes in v2:
time: 30.9 us; the launch traced here: 30.7 us
  Pallas kernels  29.3 us (95%)
  local copies, waits for them, and re-layouts  1.38 us (4%)
    pallas_call x1, Pallas kernels, shards(): pl.pallas_call(functools.partial(kernel, blocks), out_shape=jax.ShapeDtyp...  29.3 us
    unnamed x1, local copies, waits for them, and re-layouts  1.38 us

profile of v2, /device:TPU:1, one launch (start us, length us, event | category | flops | bytes accessed | tf_op | source)
XLA Modules:
  0.0 30.7 jit_solution(5751697694960499371)
XLA Ops:
  0.0 29.3 %hyena.1 = bf16[32,512]{1,0:T(8,128)(2,1)} custom-call(bf16[3,32,512]{2,1,0:T(8,128)(2,1)} %proj.1, f32[3,3,32]{2,1,0:T(4,128)} %bitcast.1, bf16[32,512]{1,0:T(8,128)(2,1)} %filt.1, f32[32]{0:T(128)} %gain.1, f32[512,256]{1,0:T(8,128)} %constant.10.clone.w1, f32[256,256]{1,0:T(8,128)} %constant.11.clone.w3, f32[256,256]{1,0:T(8,128)} %constant.12.clone.w4, ...), custom_call_target="tpu_custom_call" | custom-call | flops 200000000 | bytes 2000000 | tf_op jit(solution)/shard_map/hyena/pallas_call | solution.py:233
  29.4 1.4 %copy.11 = bf16[32,512]{1,0:T(8,128)(2,1)} copy(bf16[32,512]{1,0:T(8,128)(2,1)} %hyena.1) | data formatting | bytes 65536

commit v3 on v2

v3 whole, which is shorter than its diff:
```python
import functools

import jax
import jax.numpy as jnp
import numpy as np
from jax import lax
from jax.experimental import pallas as pl
from jax.experimental.pallas import tpu as pltpu
from jax.sharding import PartitionSpec as P

MESH = pl.DeviceIdType.MESH
LANES = 128
GROUP = 8
f32 = jnp.float32
bf16 = jnp.bfloat16


def tables(blocks, pieces):
    rows = blocks * pieces
    n = rows * LANES
    order = (np.arange(blocks)[None, :] * pieces + np.arange(pieces)[:, None]).reshape(-1)
    k1 = np.arange(rows) + 0.25
    first = np.exp(-2j * np.pi * np.outer(k1, order) / rows)
    turn = np.exp(-2j * np.pi * np.outer(k1, np.arange(LANES)) / n)
    second = np.exp(-2j * np.pi * np.outer(np.arange(LANES), np.arange(LANES)) / LANES)
    back = np.conj(second)
    last = np.conj(first).T / n
    w1 = np.concatenate([first.real, first.imag], 0)
    w3 = np.block([[second.real, second.imag], [-second.imag, second.real]])
    w4 = np.block([[back.real, back.imag], [-back.imag, back.real]])
    w6 = np.concatenate([last.real, -last.imag], 1)
    tw = np.stack([turn.real, turn.imag])
    return tuple(x.astype(np.float32) for x in (w1, w3, w4, w6, tw))


def dot(a, b):
    return jnp.dot(a, b, preferred_element_type=f32)


def kernel(
    blocks, proj, weight, filt, gain, w1, w3, w4, w6, tw, out,
    proj_v, filt_v, weight_v, gain_s, w1_v, w3_v, w4_v, w6_v, tw_v,
    halo, taps_v, query_v, spread, msg, inbox, opened, result, reply_v, back, back_f,
    load_sem, const_sem, ready, halo_send, halo_recv, send_sem, recv_sem, send2_sem, recv2_sem,
):
    chans = proj.shape[1]
    pieces = proj.shape[2] // LANES
    rows = blocks * pieces
    me = lax.axis_index("seq")
    group, place = me // (2 * GROUP), lax.rem(me, 2 * GROUP)
    holder = place < GROUP
    mine = group * GROUP + lax.rem(place, GROUP)
    groups = blocks // (2 * GROUP)

    def home(ch):
        return (ch // GROUP) * (2 * GROUP) + lax.rem(ch, GROUP)

    def tile(r):
        return slice(LANES * r, LANES * (r + 1))

    loads = [
        pltpu.make_async_copy(src, dst, load_sem.at[i])
        for i, (src, dst) in enumerate([(filt, filt_v), (proj, proj_v), (weight, weight_v), (gain, gain_s)])
    ]
    for load in loads:
        load.start()
    consts = [
        pltpu.make_async_copy(src, dst, const_sem.at[i])
        for i, (src, dst) in enumerate([(w1, w1_v), (w3, w3_v), (w4, w4_v), (w6, w6_v), (tw, tw_v)])
    ]

    barrier = pltpu.get_barrier_semaphore()

    @pl.when(holder)
    def _():
        def greet(i, carry):
            pl.semaphore_signal(
                barrier, inc=1, device_id={"seq": lax.rem(me + i, blocks)}, device_id_type=MESH
            )
            return carry

        lax.fori_loop(1, blocks, greet, 0)

    @pl.when(jnp.logical_and(place >= GROUP, place < 2 * GROUP - 1))
    def _():
        pl.semaphore_signal(barrier, inc=1, device_id={"seq": me + 1}, device_id_type=MESH)

    @pl.when(holder)
    def _():
        for const in consts:
            const.start()

    @pl.when(me == 0)
    def _():
        halo[...] = jnp.zeros_like(halo)

    after = me + 1
    pl.semaphore_wait(barrier, jnp.where(holder, chans - 1, jnp.where(place > GROUP, chans + 1, chans)))

    @pl.when(jnp.logical_not(holder))
    def _():
        pl.semaphore_signal(ready, inc=1, device_id={"seq": me - 1}, device_id_type=MESH)

    loads[0].wait()
    for r in range(pieces):
        spread[pl.ds(2 * pieces + r, chans, stride=3 * pieces), :] = filt_v[:, tile(r)].astype(f32)
    loads[1].wait()
    for j in range(2):
        for r in range(pieces):
            spread[pl.ds(j * pieces + r, chans, stride=3 * pieces), :] = proj_v[1 + j, :, tile(r)].astype(f32)
    msg[...] = spread[...].reshape(chans, 3, pieces, LANES).astype(bf16)

    def send(i, carry):
        ch = lax.rem(mine + i, chans)
        pltpu.make_async_remote_copy(
            src_ref=msg.at[ch],
            dst_ref=inbox.at[me],
            send_sem=send_sem,
            recv_sem=recv_sem,
            device_id={"seq": home(ch)},
            device_id_type=MESH,
        ).start()
        return carry

    @pl.when(jnp.logical_not(holder))
    def _():
        send(0, 0)

    lax.fori_loop(1, chans, send, 0)
    edge = pltpu.make_async_remote_copy(
        src_ref=proj_v.at[0, :, pl.ds((pieces - 1) * LANES, LANES)],
        dst_ref=halo,
        send_sem=halo_send,
        recv_sem=halo_recv,
        device_id={"seq": jnp.minimum(after, blocks - 1)},
        device_id_type=MESH,
    )

    @pl.when(jnp.logical_and(place >= GROUP - 1, place < 2 * GROUP - 1))
    def _():
        pl.semaphore_wait(ready, 1)

    @pl.when(after < blocks)
    def _():
        edge.start()

    loads[2].wait()
    for j in range(3):
        taps_v[3 * j : 3 * j + 3, :chans] = weight_v[j]
    taps_t = taps_v[...].T[:chans]
    lane = lax.broadcasted_iota(jnp.int32, (blocks, LANES), 1)

    def short(now, before, taps):
        one = pltpu.roll(jnp.where(lane[: now.shape[0]] >= LANES - 1, before, now), 1, 1)
        two = pltpu.roll(jnp.where(lane[: now.shape[0]] >= LANES - 2, before, now), 2, 1)
        total = taps[0] * two
        total = total + taps[1] * one
        total = total + taps[2] * now
        return total.astype(bf16).astype(f32)

    for r in reversed(range(pieces)):
        if r == 0:

            @pl.when(me > 0)
            def _():
                edge.wait_recv()

        now = proj_v[0, :, tile(r)].astype(f32)
        before = (halo[...] if r == 0 else proj_v[0, :, tile(r - 1)]).astype(f32)
        query_v[:, tile(r)] = short(now, before, [taps_t[:, i : i + 1] for i in range(3)])

    loads[3].wait()

    @pl.when(holder)
    def _():
        inbox[me] = msg[mine]
        for const in consts:
            const.wait()
        others = inbox.at[pl.ds(0, blocks - 1)]
        pltpu.make_async_copy(others, others, recv_sem).wait()
        opened[...] = inbox[...].astype(f32).reshape(blocks * 3 * pieces, LANES)
        part = [
            [opened[pl.ds(j * pieces + r, blocks, stride=3 * pieces), :] for r in range(pieces)]
            for j in range(3)
        ]
        chan_lane = lax.broadcasted_iota(jnp.int32, weight_v.shape[1:], 1)
        row = lax.broadcasted_iota(jnp.int32, (blocks, LANES), 0)
        conv = []
        for j in range(2):
            taps = jnp.sum(jnp.where(chan_lane == mine, weight_v[1 + j], 0.0), axis=1, keepdims=True)
            taps = [taps[i : i + 1, :] for i in range(3)]
            before = jnp.where(row == 0, 0.0, pltpu.roll(part[j][pieces - 1], 1, 0))
            done = []
            for r in range(pieces):
                done.append(short(part[j][r], before, taps))
                before = part[j][r]
            conv.append(jnp.concatenate(done, 0))
        mixed = (conv[0] * conv[1]).astype(bf16)
        both = jnp.concatenate([mixed, jnp.concatenate(part[2], 0).astype(bf16)], 1)
        step = dot(w1_v[...].astype(bf16), both)
        tr, ti = tw_v[0], tw_v[1]
        turned = []
        for half in (tile(0), tile(1)):
            re, im = step[:rows, half], step[rows:, half]
            turned.append(jnp.concatenate([re * tr - im * ti, re * ti + im * tr], 1).astype(bf16))
        spec = dot(jnp.concatenate(turned, 0), w3_v[...].astype(bf16))
        xr, xi = spec[:rows, :LANES], spec[:rows, LANES:]
        hr, hi = spec[rows:, :LANES], spec[rows:, LANES:]
        prod = jnp.concatenate([xr * hr - xi * hi, xr * hi + xi * hr], 1).astype(bf16)
        inv = dot(prod, w4_v[...].astype(bf16))
        re, im = inv[:, :LANES], inv[:, LANES:]
        untwist = jnp.concatenate([re * tr + im * ti, im * tr - re * ti], 0).astype(bf16)
        long_out = dot(w6_v[...].astype(bf16), untwist) + gain_s[mine] * mixed.astype(f32)
        for r in range(pieces):
            result[pl.ds(r, blocks, stride=pieces), :] = long_out[r * blocks : (r + 1) * blocks]
        reply_v[...] = result[...].reshape(blocks, pieces, LANES).astype(bf16)
        back[mine] = reply_v[me]

        def reply(i, carry):
            a = lax.rem(i + group, groups) * (2 * GROUP) + i // groups

            @pl.when(a != me)
            def _():
                pltpu.make_async_remote_copy(
                    src_ref=reply_v.at[a],
                    dst_ref=back.at[mine],
                    send_sem=send2_sem,
                    recv_sem=recv2_sem,
                    device_id={"seq": a},
                    device_id_type=MESH,
                ).start()

            return carry

        lax.fori_loop(0, blocks, reply, 0)
        others = back.at[pl.ds(0, chans - 1)]
        pltpu.make_async_copy(others, others, recv2_sem).wait()

    @pl.when(jnp.logical_not(holder))
    def _():
        pltpu.make_async_copy(back, back, recv2_sem).wait()

    back_f[...] = back[...].astype(f32).reshape(chans * pieces, LANES)
    for r in range(pieces):
        long_out = back_f[pl.ds(r, chans, stride=pieces), :]
        out[:, tile(r)] = (query_v[:, tile(r)] * long_out).astype(bf16)

    @pl.when(after < blocks)
    def _():
        edge.wait_send()

    @pl.when(holder)
    def _():
        sent = msg.at[pl.ds(0, chans - 1)]
        pltpu.make_async_copy(sent, sent, send_sem).wait()
        sent = reply_v.at[pl.ds(0, blocks - 1)]
        pltpu.make_async_copy(sent, sent, send2_sem).wait()

    @pl.when(jnp.logical_not(holder))
    def _():
        pltpu.make_async_copy(msg, msg, send_sem).wait()


def shards(blocks, projections, short_weight, long_filter, skip_gain):
    _, chans, tokens = projections.shape
    pieces = tokens // LANES
    rows = blocks * pieces
    consts = [jnp.asarray(x) for x in tables(blocks, pieces)]
    weight = jnp.transpose(short_weight, (0, 2, 1))
    dma = pltpu.SemaphoreType.DMA
    scratch = [
        pltpu.VMEM(projections.shape, bf16),
        pltpu.VMEM(long_filter.shape, bf16),
        pltpu.VMEM(weight.shape, f32),
        pltpu.SMEM(skip_gain.shape, f32),
        *[pltpu.VMEM(x.shape, x.dtype) for x in consts],
        pltpu.VMEM((chans, LANES), bf16),
        pltpu.VMEM((16, LANES), f32),
        pltpu.VMEM((chans, tokens), f32),
        pltpu.VMEM((chans * 3 * pieces, LANES), f32),
        pltpu.VMEM((chans, 3, pieces, LANES), bf16),
        pltpu.VMEM((blocks, 3, pieces, LANES), bf16),
        pltpu.VMEM((blocks * 3 * pieces, LANES), f32),
        pltpu.VMEM((rows, LANES), f32),
        pltpu.VMEM((blocks, pieces, LANES), bf16),
        pltpu.VMEM((chans, pieces, LANES), bf16),
        pltpu.VMEM((chans * pieces, LANES), f32),
        dma((4,)), dma((5,)), pltpu.SemaphoreType.REGULAR, dma, dma, dma, dma, dma, dma,
    ]
    return pl.pallas_call(
        functools.partial(kernel, blocks),
        out_shape=pltpu.VMEM((chans, tokens), bf16),
        in_specs=[pl.BlockSpec(memory_space=pl.ANY)] * 9,
        out_specs=pl.BlockSpec(memory_space=pltpu.VMEM),
        scratch_shapes=scratch,
        compiler_params=pltpu.CompilerParams(
            collective_id=0, has_side_effects=True, vmem_limit_bytes=56 * 1024 * 1024
        ),
        cost_estimate=pl.CostEstimate(flops=200_000_000, bytes_accessed=2_000_000, transcendentals=0),
        name="hyena",
    )(projections, weight, long_filter, skip_gain, *consts)


def solution(mesh):
    in_specs = (P(None, "chan", "seq"), P(None, "chan", None), P("chan", "seq"), P("chan"))
    out_specs = P("chan", "seq")
    body = functools.partial(shards, mesh.shape["seq"])
    return jax.shard_map(body, mesh=mesh, in_specs=in_specs, out_specs=out_specs, check_vma=False)
```

time: 30.9 us -> 26.4 us (0.85)
  Pallas kernels: 29.3 us -> 25.7 us
  local copies, waits for them, and re-layouts: 1.38 us -> 0.62 us
    pallas_call x1, Pallas kernels: 29.3 us -> 25.7 us  [shards(): pl.pallas_call(functools.partial(kernel, blocks), out_shape=pltpu.VMEM((c...]
    unnamed x1, local copies, waits for them, and re-layouts: 1.38 us -> 0.62 us
where the time goes in v3:
time: 26.4 us; the launch traced here: 26.3 us
  Pallas kernels  25.7 us (97%)
  local copies, waits for them, and re-layouts  0.62 us (2%)
    pallas_call x1, Pallas kernels, shards(): pl.pallas_call(functools.partial(kernel, blocks), out_shape=pltpu.VMEM((c...  25.7 us
    unnamed x1, local copies, waits for them, and re-layouts  0.62 us

profile of v3, /device:TPU:1, one launch (start us, length us, event | category | flops | bytes accessed | tf_op | source)
XLA Modules:
  0.0 26.3 jit_solution(12400721367193715408)
XLA Ops:
  0.0 25.7 %hyena.1 = bf16[32,512]{1,0:T(8,128)(2,1)S(1)} custom-call(bf16[3,32,512]{2,1,0:T(8,128)(2,1)} %proj.1, f32[3,3,32]{2,1,0:T(4,128)} %bitcast.1, bf16[32,512]{1,0:T(8,128)(2,1)} %filt.1, f32[32]{0:T(128)} %gain.1, f32[512,256]{1,0:T(8,128)} %constant.10.clone.w1, f32[256,256]{1,0:T(8,128)} %constant.11.clone.w3, f32[256,256]{1,0:T(8,128)} %constant.12.clone.w4, ...), custom_call_target="tpu_custom_call" | custom-call | flops 200000000 | bytes 2000000 | tf_op jit(solution)/shard_map/hyena/pallas_call | solution.py:290
  25.7 0.6 %copy.11 = bf16[32,512]{1,0:T(8,128)(2,1)} copy(bf16[32,512]{1,0:T(8,128)(2,1)S(1)} %hyena.1) | data formatting | bytes 65536

commit v4 on v3

v4 whole, which is shorter than its diff:
```python
import functools

import jax
import jax.numpy as jnp
import numpy as np
from jax import lax
from jax.experimental import pallas as pl
from jax.experimental.pallas import tpu as pltpu
from jax.sharding import PartitionSpec as P

MESH = pl.DeviceIdType.MESH
LANES = 128
ROW = 16
FIRST, STEP, COUNT = 1, 1, 2
f32 = jnp.float32
bf16 = jnp.bfloat16


def tables(blocks, pieces):
    rows = blocks * pieces
    n = rows * LANES
    order = (np.arange(blocks)[None, :] * pieces + np.arange(pieces)[:, None]).reshape(-1)
    k1 = np.arange(rows) + 0.25
    first = np.exp(-2j * np.pi * np.outer(k1, order) / rows)
    turn = np.exp(-2j * np.pi * np.outer(k1, np.arange(LANES)) / n)
    second = np.exp(-2j * np.pi * np.outer(np.arange(LANES), np.arange(LANES)) / LANES)
    back = np.conj(second)
    last = np.conj(first).T / n
    w1 = np.concatenate([first.real, first.imag], 0)
    w3 = np.block([[second.real, second.imag], [-second.imag, second.real]])
    w4 = np.block([[back.real, back.imag], [-back.imag, back.real]])
    w6 = np.concatenate([last.real, -last.imag], 1)
    tw = np.stack([turn.real, turn.imag])
    return tuple(x.astype(np.float32) for x in (w1, w3, w4, w6, tw))


def dot(a, b):
    return jnp.dot(a, b, preferred_element_type=f32)


def kernel(
    blocks, proj, weight, filt, gain, w1, w3, w4, w6, tw, out,
    proj_v, filt_v, weight_v, gain_s, w1_v, w3_v, w4_v, w6_v, tw_v,
    halo, taps_v, query_v, filt_s, mix_s, filt_m, mix_m, edge_m, filt_in, mix_in, edge_in, filt_o, mix_o, edge_o, spec_h,
    result, reply_v, back, back_f,
    load_sem, const_sem, ready, halo_send, halo_recv, filt_send, filt_recv, mix_send, mix_recv, edge_send, edge_recv, send2_sem, recv2_sem,
):
    chans = proj.shape[1]
    pieces = proj.shape[2] // LANES
    rows = blocks * pieces
    me = lax.axis_index("seq")
    groups = blocks // ROW
    homes = groups * 2 * COUNT
    each = chans // homes
    group, place = me // ROW, lax.rem(me, ROW)

    def holds(seq):
        chip = lax.rem(seq, ROW) // 2 - FIRST
        return (chip >= 0) & (chip < STEP * COUNT) & (lax.rem(chip + STEP * ROW, STEP) == 0)

    def home(h):
        slot = lax.rem(h, 2 * COUNT)
        return (h // (2 * COUNT)) * ROW + 2 * (FIRST + STEP * (slot // 2)) + lax.rem(slot, 2)

    holder = holds(me)
    slot = 2 * ((place // 2 - FIRST) // STEP) + lax.rem(place, 2)
    mine = group * (2 * COUNT) + jnp.where(holder, slot, lax.rem(place, 2 * COUNT))

    def tile(r):
        return slice(LANES * r, LANES * (r + 1))

    loads = [
        pltpu.make_async_copy(src, dst, load_sem.at[i])
        for i, (src, dst) in enumerate([(weight, weight_v), (filt, filt_v), (proj, proj_v), (gain, gain_s)])
    ]
    for load in loads:
        load.start()
    consts = [
        pltpu.make_async_copy(src, dst, const_sem.at[i])
        for i, (src, dst) in enumerate([(w1, w1_v), (w3, w3_v), (w4, w4_v), (w6, w6_v), (tw, tw_v)])
    ]

    barrier = pltpu.get_barrier_semaphore()

    @pl.when(holder)
    def _():
        def greet(i, carry):
            a = lax.rem(i + group, groups) * ROW + i // groups

            @pl.when(a != me)
            def _():
                pl.semaphore_signal(barrier, inc=1, device_id={"seq": a}, device_id_type=MESH)

            return carry

        lax.fori_loop(0, blocks, greet, 0)

    after = me + 1
    bare = jnp.logical_not(holder)
    next_bare = (after < blocks) & jnp.logical_not(holds(after))
    last_bare = (me > 0) & jnp.logical_not(holds(me - 1))
    row_start, row_end = place == 0, place == ROW - 1

    @pl.when(bare & next_bare & jnp.logical_not(row_end))
    def _():
        pl.semaphore_signal(barrier, inc=1, device_id={"seq": after}, device_id_type=MESH)

    @pl.when(bare & row_start & (me > 0))
    def _():
        pl.semaphore_signal(barrier, inc=1, device_id={"seq": me - 1}, device_id_type=MESH)

    @pl.when(holder)
    def _():
        for const in consts:
            const.start()

    @pl.when(me == 0)
    def _():
        halo[...] = jnp.zeros_like(halo)

    greeted = [bare & last_bare & jnp.logical_not(row_start), next_bare & row_end]
    pl.semaphore_wait(barrier, homes - holder.astype(jnp.int32) + sum(x.astype(jnp.int32) for x in greeted))

    @pl.when(bare & jnp.logical_not(row_start))
    def _():
        pl.semaphore_signal(ready, inc=1, device_id={"seq": me - 1}, device_id_type=MESH)

    def far_first(i):
        return lax.rem(group + jnp.where(i == 0, 2, jnp.where(i == groups - 1, 0, 2 * i - 1)), groups)

    def send(src, each, dst, send_sem, recv_sem):
        def one(i, carry):
            slot = lax.rem(i, 2 * COUNT)
            slot = jnp.where(place >= ROW * 3 // 4, 2 * COUNT - 1 - slot, slot)
            h = far_first(i // (2 * COUNT)) * (2 * COUNT) + slot

            @pl.when(home(h) != me)
            def _():
                pltpu.make_async_remote_copy(
                    src_ref=src.at[pl.ds(h * each, each)],
                    dst_ref=dst.at[pl.ds(me * each, each)],
                    send_sem=send_sem,
                    recv_sem=recv_sem,
                    device_id={"seq": home(h)},
                    device_id_type=MESH,
                ).start()

            return carry

        lax.fori_loop(0, homes, one, 0)

    lane = lax.broadcasted_iota(jnp.int32, (blocks, LANES), 1)

    def short(now, before, taps):
        one = pltpu.roll(jnp.where(lane[: now.shape[0]] >= LANES - 1, before, now), 1, 1)
        two = pltpu.roll(jnp.where(lane[: now.shape[0]] >= LANES - 2, before, now), 2, 1)
        total = taps[0] * two
        total = total + taps[1] * one
        total = total + taps[2] * now
        return total.astype(bf16).astype(f32)

    loads[0].wait()
    for j in range(3):
        taps_v[3 * j : 3 * j + 3, :chans] = weight_v[j]
    taps_t = taps_v[...].T[:chans]
    taps = [[taps_t[:, 3 * j + i : 3 * j + i + 1] for i in range(3)] for j in range(3)]

    loads[1].wait()
    for r in range(pieces):
        filt_s[pl.ds(r, chans, stride=pieces), :] = filt_v[:, tile(r)].astype(f32)
    filt_m[...] = filt_s[...].reshape(chans, pieces, LANES).astype(bf16)
    send(filt_m, each, filt_in, filt_send, filt_recv)

    loads[2].wait()
    here = lane[:chans]
    ends = []
    for j in (1, 2):
        head, tail = proj_v[j, :, tile(0)].astype(f32), proj_v[j, :, tile(pieces - 1)].astype(f32)
        ends.append(jnp.where(here < LANES // 2, head, tail))
    ends = jnp.where((here >= 6) & (here < 10), pltpu.roll(ends[1], 8, 1), ends[0])
    edge_m[...] = ends.reshape(homes, each, LANES).astype(bf16)
    send(edge_m, 1, edge_in, edge_send, edge_recv)

    for r in range(pieces):
        conv = []
        for j in (1, 2):
            now = proj_v[j, :, tile(r)].astype(f32)
            before = proj_v[j, :, tile(max(r - 1, 0))].astype(f32)
            conv.append(short(now, before, taps[j]))
        mix_s[pl.ds(r, chans, stride=pieces), :] = conv[0] * conv[1]
    mix_m[...] = mix_s[...].reshape(chans, pieces, LANES).astype(bf16)
    send(mix_m, each, mix_in, mix_send, mix_recv)

    edge = pltpu.make_async_remote_copy(
        src_ref=proj_v.at[0, :, pl.ds((pieces - 1) * LANES, LANES)],
        dst_ref=halo,
        send_sem=halo_send,
        recv_sem=halo_recv,
        device_id={"seq": jnp.minimum(after, blocks - 1)},
        device_id_type=MESH,
    )

    @pl.when(next_bare & jnp.logical_not(row_end))
    def _():
        pl.semaphore_wait(ready, 1)

    @pl.when(after < blocks)
    def _():
        edge.start()

    for r in reversed(range(pieces)):
        if r == 0:

            @pl.when(me > 0)
            def _():
                edge.wait_recv()

        now = proj_v[0, :, tile(r)].astype(f32)
        before = (halo[...] if r == 0 else proj_v[0, :, tile(r - 1)]).astype(f32)
        query_v[:, tile(r)] = short(now, before, taps[0])

    loads[3].wait()

    @pl.when(holder)
    def _():
        for const in consts:
            const.wait()
        tr, ti = tw_v[0], tw_v[1]

        def forward(signals):
            step = dot(w1_v[...].astype(bf16), jnp.concatenate(signals, 1))
            turned = []
            for e in range(each):
                re, im = step[:rows, tile(e)], step[rows:, tile(e)]
                turned.append(jnp.concatenate([re * tr - im * ti, re * ti + im * tr], 1).astype(bf16))
            return dot(jnp.concatenate(turned, 0), w3_v[...].astype(bf16))

        def arrived(dst, each, sem):
            others = dst.at[pl.ds(0, (blocks - 1) * each)]
            pltpu.make_async_copy(others, others, sem).wait()

        for src, dst in ((filt_m, filt_in), (mix_m, mix_in)):
            dst[pl.ds(me * each, each)] = src[pl.ds(mine * each, each)]
        edge_in[me] = edge_m[mine]
        arrived(filt_in, each, filt_recv)
        filt_o[...] = filt_in[...].astype(f32).reshape(blocks * each * pieces, LANES)

        def rows_of(opened, e):
            return [opened[pl.ds(e * pieces + r, blocks, stride=each * pieces), :] for r in range(pieces)]

        spec_h[...] = forward([jnp.concatenate(rows_of(filt_o, e), 0).astype(bf16) for e in range(each)])
        arrived(edge_in, 1, edge_recv)
        edge_o[...] = edge_in[...].astype(f32).reshape(blocks * each, LANES)
        chan_lane = lax.broadcasted_iota(jnp.int32, weight_v.shape[1:], 1)
        row = lax.broadcasted_iota(jnp.int32, (blocks, LANES), 0)
        heads = []
        for e in range(each):
            ends = edge_o[pl.ds(e, blocks, stride=each), :]
            conv = []
            for j in (1, 2):
                now = ends if j == 1 else pltpu.roll(ends, LANES - 8, 1)
                before = jnp.where(row == 0, 0.0, pltpu.roll(now, 1, 0))
                held = jnp.sum(
                    jnp.where(chan_lane == mine * each + e, weight_v[j], 0.0), axis=1, keepdims=True
                )
                conv.append(short(now, before, [held[i : i + 1, :] for i in range(3)]))
            heads.append((conv[0] * conv[1]).astype(bf16).astype(f32))
        arrived(mix_in, each, mix_recv)
        mix_o[...] = mix_in[...].astype(f32).reshape(blocks * each * pieces, LANES)
        mixes = []
        for e in range(each):
            part = rows_of(mix_o, e)
            part[0] = jnp.where(lane < 2, heads[e], part[0])
            mixes.append(jnp.concatenate(part, 0).astype(bf16))
        spec = forward(mixes)
        prods = []
        for e in range(each):
            x, h = spec[e * rows : (e + 1) * rows], spec_h[e * rows : (e + 1) * rows]
            xr, xi, hr, hi = x[:, :LANES], x[:, LANES:], h[:, :LANES], h[:, LANES:]
            prods.append(jnp.concatenate([xr * hr - xi * hi, xr * hi + xi * hr], 1).astype(bf16))
        inv = dot(jnp.concatenate(prods, 0), w4_v[...].astype(bf16))
        untwist = []
        for e in range(each):
            part = inv[e * rows : (e + 1) * rows]
            re, im = part[:, :LANES], part[:, LANES:]
            untwist.append(jnp.concatenate([re * tr + im * ti, im * tr - re * ti], 0).astype(bf16))
        long_out = dot(w6_v[...].astype(bf16), jnp.concatenate(untwist, 1))
        for e in range(each):
            total = long_out[:, tile(e)] + gain_s[mine * each + e] * mixes[e].astype(f32)
            for r in range(pieces):
                result[pl.ds(e * pieces + r, blocks, stride=each * pieces), :] = total[
                    r * blocks : (r + 1) * blocks
                ]
        reply_v[...] = result[...].reshape(blocks, each, pieces, LANES).astype(bf16)
        back[pl.ds(mine * each, each)] = reply_v[me]

        def reply(i, carry):
            a = far_first(lax.rem(i, groups)) * ROW + i // groups

            @pl.when(a != me)
            def _():
                pltpu.make_async_remote_copy(
                    src_ref=reply_v.at[a],
                    dst_ref=back.at[pl.ds(mine * each, each)],
                    send_sem=send2_sem,
                    recv_sem=recv2_sem,
                    device_id={"seq": a},
                    device_id_type=MESH,
                ).start()

            return carry

        lax.fori_loop(0, blocks, reply, 0)
        others = back.at[pl.ds(0, chans - each)]
        pltpu.make_async_copy(others, others, recv2_sem).wait()

    @pl.when(jnp.logical_not(holder))
    def _():
        pltpu.make_async_copy(back, back, recv2_sem).wait()

    back_f[...] = back[...].astype(f32).reshape(chans * pieces, LANES)
    for r in range(pieces):
        long_out = back_f[pl.ds(r, chans, stride=pieces), :]
        out[:, tile(r)] = (query_v[:, tile(r)] * long_out).astype(bf16)

    @pl.when(after < blocks)
    def _():
        edge.wait_send()

    sends = ((filt_m, each, filt_send), (mix_m, each, mix_send), (edge_m, 1, edge_send))

    @pl.when(holder)
    def _():
        for src, step, sem in sends:
            sent = src.at[pl.ds(0, (homes - 1) * step)]
            pltpu.make_async_copy(sent, sent, sem).wait()
        sent = reply_v.at[pl.ds(0, blocks - 1)]
        pltpu.make_async_copy(sent, sent, send2_sem).wait()

    @pl.when(jnp.logical_not(holder))
    def _():
        for src, _, sem in sends:
            pltpu.make_async_copy(src, src, sem).wait()


def shards(blocks, projections, short_weight, long_filter, skip_gain):
    _, chans, tokens = projections.shape
    pieces = tokens // LANES
    each = chans // (blocks // ROW * 2 * COUNT)
    rows = blocks * pieces
    consts = [jnp.asarray(x) for x in tables(blocks, pieces)]
    weight = jnp.transpose(short_weight, (0, 2, 1))
    dma = pltpu.SemaphoreType.DMA
    scratch = [
        pltpu.VMEM(projections.shape, bf16),
        pltpu.VMEM(long_filter.shape, bf16),
        pltpu.VMEM(weight.shape, f32),
        pltpu.SMEM(skip_gain.shape, f32),
        *[pltpu.VMEM(x.shape, x.dtype) for x in consts],
        pltpu.VMEM((chans, LANES), bf16),
        pltpu.VMEM((16, LANES), f32),
        pltpu.VMEM((chans, tokens), f32),
        pltpu.VMEM((chans * pieces, LANES), f32),
        pltpu.VMEM((chans * pieces, LANES), f32),
        pltpu.VMEM((chans, pieces, LANES), bf16),
        pltpu.VMEM((chans, pieces, LANES), bf16),
        pltpu.VMEM((chans // each, each, LANES), bf16),
        pltpu.VMEM((blocks * each, pieces, LANES), bf16),
        pltpu.VMEM((blocks * each, pieces, LANES), bf16),
        pltpu.VMEM((blocks, each, LANES), bf16),
        pltpu.VMEM((blocks * each * pieces, LANES), f32),
        pltpu.VMEM((blocks * each * pieces, LANES), f32),
        pltpu.VMEM((blocks * each, LANES), f32),
        pltpu.VMEM((each * rows, 2 * LANES), f32),
        pltpu.VMEM((rows * each, LANES), f32),
        pltpu.VMEM((blocks, each, pieces, LANES), bf16),
        pltpu.VMEM((chans, pieces, LANES), bf16),
        pltpu.VMEM((chans * pieces, LANES), f32),
        dma((4,)), dma((5,)), pltpu.SemaphoreType.REGULAR, *[dma] * 10,
    ]
    return pl.pallas_call(
        functools.partial(kernel, blocks),
        out_shape=pltpu.VMEM((chans, tokens), bf16),
        in_specs=[pl.BlockSpec(memory_space=pl.ANY)] * 9,
        out_specs=pl.BlockSpec(memory_space=pltpu.VMEM),
        scratch_shapes=scratch,
        compiler_params=pltpu.CompilerParams(
            collective_id=0, has_side_effects=True, vmem_limit_bytes=56 * 1024 * 1024
        ),
        cost_estimate=pl.CostEstimate(flops=200_000_000, bytes_accessed=2_000_000, transcendentals=0),
        name="hyena",
    )(projections, weight, long_filter, skip_gain, *consts)


def solution(mesh):
    in_specs = (P(None, "chan", "seq"), P(None, "chan", None), P("chan", "seq"), P("chan"))
    out_specs = P("chan", "seq")
    body = functools.partial(shards, mesh.shape["seq"])
    return jax.shard_map(body, mesh=mesh, in_specs=in_specs, out_specs=out_specs, check_vma=False)
```

time: 26.4 us -> 24.9 us (0.943)
  Pallas kernels: 25.7 us -> 24.2 us
    pallas_call x1, Pallas kernels: 25.7 us -> 24.2 us  [shards(): pl.pallas_call(functools.partial(kernel, blocks), out_shape=pltpu.VMEM((c...]
where the time goes in v4:
time: 24.9 us; the launch traced here: 24.8 us
  Pallas kernels  24.2 us (97%)
  local copies, waits for them, and re-layouts  0.62 us (2%)
    pallas_call x1, Pallas kernels, shards(): pl.pallas_call(functools.partial(kernel, blocks), out_shape=pltpu.VMEM((c...  24.2 us
    unnamed x1, local copies, waits for them, and re-layouts  0.62 us

profile of v4, /device:TPU:1, one launch (start us, length us, event | category | flops | bytes accessed | tf_op | source)
XLA Modules:
  0.0 24.8 jit_solution(10051858407306491203)
XLA Ops:
  0.0 24.2 %hyena.1 = bf16[32,512]{1,0:T(8,128)(2,1)S(1)} custom-call(bf16[3,32,512]{2,1,0:T(8,128)(2,1)} %proj.1, f32[3,3,32]{2,1,0:T(4,128)} %bitcast.1, bf16[32,512]{1,0:T(8,128)(2,1)} %filt.1, f32[32]{0:T(128)} %gain.1, f32[512,256]{1,0:T(8,128)} %constant.10.clone.w1, f32[256,256]{1,0:T(8,128)} %constant.11.clone.w3, f32[256,256]{1,0:T(8,128)} %constant.12.clone.w4, ...), custom_call_target="tpu_custom_call" | custom-call | flops 200000000 | bytes 2000000 | tf_op jit(solution)/shard_map/hyena/pallas_call | solution.py:381
  24.2 0.6 %copy.11 = bf16[32,512]{1,0:T(8,128)(2,1)} copy(bf16[32,512]{1,0:T(8,128)(2,1)S(1)} %hyena.1) | data formatting | bytes 65536

commit v5 on v4

--- a/solution.py
+++ b/solution.py
@@ -11,7 +11,8 @@
 MESH = pl.DeviceIdType.MESH
 LANES = 128
 ROW = 16
-FIRST, STEP, COUNT = 1, 1, 2
+FIRST, COUNT = 1, 1
+GREET = (5, 6, 4, 7, 3, 0, 2, 1)
 f32 = jnp.float32
 bf16 = jnp.bfloat16
 
@@ -42,6 +43,7 @@
     blocks, proj, weight, filt, gain, w1, w3, w4, w6, tw, out,
     proj_v, filt_v, weight_v, gain_s, w1_v, w3_v, w4_v, w6_v, tw_v,
     halo, taps_v, query_v, filt_s, mix_s, filt_m, mix_m, edge_m, filt_in, mix_in, edge_in, filt_o, mix_o, edge_o, spec_h,
+    w1_b, w3_b, w4_b, w6_b,
     result, reply_v, back, back_f,
     load_sem, const_sem, ready, halo_send, halo_recv, filt_send, filt_recv, mix_send, mix_recv, edge_send, edge_recv, send2_sem, recv2_sem,
 ):
@@ -54,17 +56,14 @@
     each = chans // homes
     group, place = me // ROW, lax.rem(me, ROW)
 
+    far_first = [lax.rem(group + step, groups) for step in (2, 1, 3, 0)[-groups:]]
+
     def holds(seq):
         chip = lax.rem(seq, ROW) // 2 - FIRST
-        return (chip >= 0) & (chip < STEP * COUNT) & (lax.rem(chip + STEP * ROW, STEP) == 0)
-
-    def home(h):
-        slot = lax.rem(h, 2 * COUNT)
-        return (h // (2 * COUNT)) * ROW + 2 * (FIRST + STEP * (slot // 2)) + lax.rem(slot, 2)
+        return (chip >= 0) & (chip < COUNT)
 
     holder = holds(me)
-    slot = 2 * ((place // 2 - FIRST) // STEP) + lax.rem(place, 2)
-    mine = group * (2 * COUNT) + jnp.where(holder, slot, lax.rem(place, 2 * COUNT))
+    mine = group * (2 * COUNT) + jnp.where(holder, place - 2 * FIRST, 0)
 
     def tile(r):
         return slice(LANES * r, LANES * (r + 1))
@@ -84,16 +83,13 @@
 
     @pl.when(holder)
     def _():
-        def greet(i, carry):
-            a = lax.rem(i + group, groups) * ROW + i // groups
-
-            @pl.when(a != me)
-            def _():
-                pl.semaphore_signal(barrier, inc=1, device_id={"seq": a}, device_id_type=MESH)
-
-            return carry
-
-        lax.fori_loop(0, blocks, greet, 0)
+        for place_to in [2 * z + c for z in GREET for c in (0, 1)]:
+            for g in far_first:
+                a = g * ROW + place_to
+
+                @pl.when(a != me)
+                def _():
+                    pl.semaphore_signal(barrier, inc=1, device_id={"seq": a}, device_id_type=MESH)
 
     after = me + 1
     bare = jnp.logical_not(holder)
@@ -125,29 +121,29 @@
     def _():
         pl.semaphore_signal(ready, inc=1, device_id={"seq": me - 1}, device_id_type=MESH)
 
-    def far_first(i):
-        return lax.rem(group + jnp.where(i == 0, 2, jnp.where(i == groups - 1, 0, 2 * i - 1)), groups)
+    half = groups // 2
+    turn_of = jnp.where((place < ROW // 2) | (group < half - 1), 0, 1)
+    spans = [[], []]
+    for g in range(groups):
+        spans[0].append(g * ROW)
+        spans[0 if g < half - 1 else 1].append(g * ROW + ROW // 2)
 
     def send(src, each, dst, send_sem, recv_sem):
-        def one(i, carry):
-            slot = lax.rem(i, 2 * COUNT)
-            slot = jnp.where(place >= ROW * 3 // 4, 2 * COUNT - 1 - slot, slot)
-            h = far_first(i // (2 * COUNT)) * (2 * COUNT) + slot
-
-            @pl.when(home(h) != me)
-            def _():
-                pltpu.make_async_remote_copy(
-                    src_ref=src.at[pl.ds(h * each, each)],
-                    dst_ref=dst.at[pl.ds(me * each, each)],
-                    send_sem=send_sem,
-                    recv_sem=recv_sem,
-                    device_id={"seq": home(h)},
-                    device_id_type=MESH,
-                ).start()
-
-            return carry
-
-        lax.fori_loop(0, homes, one, 0)
+        for g in far_first:
+            for k in range(2 * COUNT):
+                slot = jnp.where(place >= ROW * 3 // 4, 2 * COUNT - 1 - k, k)
+                h, to = g * (2 * COUNT) + slot, g * ROW + 2 * FIRST + slot
+
+                @pl.when(to != me)
+                def _():
+                    pltpu.make_async_remote_copy(
+                        src_ref=src.at[pl.ds(h * each, each)],
+                        dst_ref=dst.at[pl.ds(me * each, each)],
+                        send_sem=send_sem,
+                        recv_sem=recv_sem.at[turn_of],
+                        device_id={"seq": to},
+                        device_id_type=MESH,
+                    ).start()
 
     lane = lax.broadcasted_iota(jnp.int32, (blocks, LANES), 1)
 
@@ -225,92 +221,100 @@
     def _():
         for const in consts:
             const.wait()
+        for src, dst in zip((w1_v, w3_v, w4_v, w6_v), (w1_b, w3_b, w4_b, w6_b)):
+            dst[...] = src[...].astype(bf16)
         tr, ti = tw_v[0], tw_v[1]
-
-        def forward(signals):
-            step = dot(w1_v[...].astype(bf16), jnp.concatenate(signals, 1))
-            turned = []
-            for e in range(each):
-                re, im = step[:rows, tile(e)], step[rows:, tile(e)]
-                turned.append(jnp.concatenate([re * tr - im * ti, re * ti + im * tr], 1).astype(bf16))
-            return dot(jnp.concatenate(turned, 0), w3_v[...].astype(bf16))
-
-        def arrived(dst, each, sem):
-            others = dst.at[pl.ds(0, (blocks - 1) * each)]
-            pltpu.make_async_copy(others, others, sem).wait()
-
+        for opened in (filt_o, mix_o, edge_o):
+            opened[...] = jnp.zeros_like(opened)
         for src, dst in ((filt_m, filt_in), (mix_m, mix_in)):
             dst[pl.ds(me * each, each)] = src[pl.ds(mine * each, each)]
         edge_in[me] = edge_m[mine]
-        arrived(filt_in, each, filt_recv)
-        filt_o[...] = filt_in[...].astype(f32).reshape(blocks * each * pieces, LANES)
+        chan_lane = lax.broadcasted_iota(jnp.int32, weight_v.shape[1:], 1)
+        row = lax.broadcasted_iota(jnp.int32, (blocks, LANES), 0)
+        held = []
+        for e in range(each):
+            here = chan_lane == mine * each + e
+            rows_j = [jnp.sum(jnp.where(here, weight_v[j], 0.0), axis=1, keepdims=True) for j in (1, 2)]
+            held.append([[x[i : i + 1, :] for i in range(3)] for x in rows_j])
+
+        def forward(signals):
+            step = dot(w1_b[...], jnp.concatenate(signals, 1))
+            turned = []
+            for e in range(each):
+                re, im = step[:rows, tile(e)], step[rows:, tile(e)]
+                turned.append(jnp.concatenate([re * tr - im * ti, re * ti + im * tr], 1).astype(bf16))
+            return dot(jnp.concatenate(turned, 0), w3_b[...])
+
+        def take(turn, src, step, lines, dst, sem):
+            count = len(spans[turn]) * (ROW // 2) - (1 if turn == 0 else 0)
+            others = src.at[pl.ds(0, count * step)]
+            pltpu.make_async_copy(others, others, sem.at[turn]).wait()
+            for a in spans[turn]:
+                b = a + ROW // 2
+                fresh = src[a * step : b * step].astype(f32)
+                dst[a * lines : b * lines, :] = fresh.reshape((b - a) * lines, LANES)
 
         def rows_of(opened, e):
             return [opened[pl.ds(e * pieces + r, blocks, stride=each * pieces), :] for r in range(pieces)]
 
-        spec_h[...] = forward([jnp.concatenate(rows_of(filt_o, e), 0).astype(bf16) for e in range(each)])
-        arrived(edge_in, 1, edge_recv)
-        edge_o[...] = edge_in[...].astype(f32).reshape(blocks * each, LANES)
-        chan_lane = lax.broadcasted_iota(jnp.int32, weight_v.shape[1:], 1)
-        row = lax.broadcasted_iota(jnp.int32, (blocks, LANES), 0)
-        heads = []
-        for e in range(each):
-            ends = edge_o[pl.ds(e, blocks, stride=each), :]
-            conv = []
-            for j in (1, 2):
-                now = ends if j == 1 else pltpu.roll(ends, LANES - 8, 1)
-                before = jnp.where(row == 0, 0.0, pltpu.roll(now, 1, 0))
-                held = jnp.sum(
-                    jnp.where(chan_lane == mine * each + e, weight_v[j], 0.0), axis=1, keepdims=True
-                )
-                conv.append(short(now, before, [held[i : i + 1, :] for i in range(3)]))
-            heads.append((conv[0] * conv[1]).astype(bf16).astype(f32))
-        arrived(mix_in, each, mix_recv)
-        mix_o[...] = mix_in[...].astype(f32).reshape(blocks * each * pieces, LANES)
-        mixes = []
-        for e in range(each):
-            part = rows_of(mix_o, e)
-            part[0] = jnp.where(lane < 2, heads[e], part[0])
-            mixes.append(jnp.concatenate(part, 0).astype(bf16))
-        spec = forward(mixes)
-        prods = []
-        for e in range(each):
-            x, h = spec[e * rows : (e + 1) * rows], spec_h[e * rows : (e + 1) * rows]
-            xr, xi, hr, hi = x[:, :LANES], x[:, LANES:], h[:, :LANES], h[:, LANES:]
-            prods.append(jnp.concatenate([xr * hr - xi * hi, xr * hi + xi * hr], 1).astype(bf16))
-        inv = dot(jnp.concatenate(prods, 0), w4_v[...].astype(bf16))
-        untwist = []
-        for e in range(each):
-            part = inv[e * rows : (e + 1) * rows]
-            re, im = part[:, :LANES], part[:, LANES:]
-            untwist.append(jnp.concatenate([re * tr + im * ti, im * tr - re * ti], 0).astype(bf16))
-        long_out = dot(w6_v[...].astype(bf16), jnp.concatenate(untwist, 1))
-        for e in range(each):
-            total = long_out[:, tile(e)] + gain_s[mine * each + e] * mixes[e].astype(f32)
-            for r in range(pieces):
-                result[pl.ds(e * pieces + r, blocks, stride=each * pieces), :] = total[
-                    r * blocks : (r + 1) * blocks
-                ]
-        reply_v[...] = result[...].reshape(blocks, each, pieces, LANES).astype(bf16)
-        back[pl.ds(mine * each, each)] = reply_v[me]
-
-        def reply(i, carry):
-            a = far_first(lax.rem(i, groups)) * ROW + i // groups
-
-            @pl.when(a != me)
+        for turn in range(2):
+            take(turn, filt_in, each, each * pieces, filt_o, filt_recv)
+            spec_h[...] = forward([jnp.concatenate(rows_of(filt_o, e), 0).astype(bf16) for e in range(each)])
+            take(turn, edge_in, 1, each, edge_o, edge_recv)
+            heads = []
+            for e in range(each):
+                ends = edge_o[pl.ds(e, blocks, stride=each), :]
+                conv = []
+                for now, taps in zip((ends, pltpu.roll(ends, LANES - 8, 1)), held[e]):
+                    conv.append(short(now, jnp.where(row == 0, 0.0, pltpu.roll(now, 1, 0)), taps))
+                heads.append((conv[0] * conv[1]).astype(bf16).astype(f32))
+            take(turn, mix_in, each, each * pieces, mix_o, mix_recv)
+            mixes = []
+            for e in range(each):
+                part = rows_of(mix_o, e)
+                part[0] = jnp.where(lane < 2, heads[e], part[0])
+                mixes.append(jnp.concatenate(part, 0).astype(bf16))
+            spec = forward(mixes)
+            prods = []
+            for e in range(each):
+                x, h = spec[e * rows : (e + 1) * rows], spec_h[e * rows : (e + 1) * rows]
+                xr, xi, hr, hi = x[:, :LANES], x[:, LANES:], h[:, :LANES], h[:, LANES:]
+                prods.append(jnp.concatenate([xr * hr - xi * hi, xr * hi + xi * hr], 1).astype(bf16))
+            inv = dot(jnp.concatenate(prods, 0), w4_b[...])
+            untwist = []
+            for e in range(each):
+                part = inv[e * rows : (e + 1) * rows]
+                re, im = part[:, :LANES], part[:, LANES:]
+                untwist.append(jnp.concatenate([re * tr + im * ti, im * tr - re * ti], 0).astype(bf16))
+            long_out = dot(w6_b[...], jnp.concatenate(untwist, 1))
+            for e in range(each):
+                total = long_out[:, tile(e)] + gain_s[mine * each + e] * mixes[e].astype(f32)
+                for r in range(pieces):
+                    result[pl.ds(e * pieces + r, blocks, stride=each * pieces), :] = total[
+                        r * blocks : (r + 1) * blocks
+                    ]
+            reply_v[turn] = result[...].reshape(blocks, each, pieces, LANES).astype(bf16)
+
+            @pl.when((group < half) if turn == 0 else (group >= half))
             def _():
-                pltpu.make_async_remote_copy(
-                    src_ref=reply_v.at[a],
-                    dst_ref=back.at[pl.ds(mine * each, each)],
-                    send_sem=send2_sem,
-                    recv_sem=recv2_sem,
-                    device_id={"seq": a},
-                    device_id_type=MESH,
-                ).start()
-
-            return carry
-
-        lax.fori_loop(0, blocks, reply, 0)
+                back[pl.ds(mine * each, each)] = reply_v[turn, me]
+
+            early = [(p, g) for p in range(ROW // 2) for g in range(groups) if (g < half) == (turn == 0)]
+            late = [(p, g) for p in range(ROW // 2, ROW) for g in range(groups) if turn == 1]
+            for place_to, g in early + late:
+                a = g * ROW + place_to
+
+                @pl.when(me != a)
+                def _():
+                    pltpu.make_async_remote_copy(
+                        src_ref=reply_v.at[turn, a],
+                        dst_ref=back.at[pl.ds(mine * each, each)],
+                        send_sem=send2_sem,
+                        recv_sem=recv2_sem,
+                        device_id={"seq": a},
+                        device_id_type=MESH,
+                    ).start()
+
         others = back.at[pl.ds(0, chans - each)]
         pltpu.make_async_copy(others, others, recv2_sem).wait()
 
@@ -334,7 +338,7 @@
         for src, step, sem in sends:
             sent = src.at[pl.ds(0, (homes - 1) * step)]
             pltpu.make_async_copy(sent, sent, sem).wait()
-        sent = reply_v.at[pl.ds(0, blocks - 1)]
+        sent = reply_v.at[0, pl.ds(0, blocks - 1)]
         pltpu.make_async_copy(sent, sent, send2_sem).wait()
 
     @pl.when(jnp.logical_not(holder))
@@ -372,11 +376,12 @@
         pltpu.VMEM((blocks * each * pieces, LANES), f32),
         pltpu.VMEM((blocks * each, LANES), f32),
         pltpu.VMEM((each * rows, 2 * LANES), f32),
+        *[pltpu.VMEM(x.shape, bf16) for x in consts[:4]],
         pltpu.VMEM((rows * each, LANES), f32),
-        pltpu.VMEM((blocks, each, pieces, LANES), bf16),
+        pltpu.VMEM((2, blocks, each, pieces, LANES), bf16),
         pltpu.VMEM((chans, pieces, LANES), bf16),
         pltpu.VMEM((chans * pieces, LANES), f32),
-        dma((4,)), dma((5,)), pltpu.SemaphoreType.REGULAR, *[dma] * 10,
+        dma((4,)), dma((5,)), pltpu.SemaphoreType.REGULAR, dma, dma, *[dma, dma((2,))] * 3, dma, dma,
     ]
     return pl.pallas_call(
         functools.partial(kernel, blocks),

time: 24.9 us -> 23.1 us (0.928)
  Pallas kernels: 24.2 us -> 22.3 us
    pallas_call x1, Pallas kernels: 24.2 us -> 22.3 us  [shards(): pl.pallas_call(functools.partial(kernel, blocks), out_shape=pltpu.VMEM((c...]
where the time goes in v5:
time: 23.1 us; the launch traced here: 22.9 us
  Pallas kernels  22.3 us (97%)
  local copies, waits for them, and re-layouts  0.62 us (3%)
    pallas_call x1, Pallas kernels, shards(): pl.pallas_call(functools.partial(kernel, blocks), out_shape=pltpu.VMEM((c...  22.3 us
    unnamed x1, local copies, waits for them, and re-layouts  0.62 us

profile of v5, /device:TPU:1, one launch (start us, length us, event | category | flops | bytes accessed | tf_op | source)
XLA Modules:
  0.0 22.9 jit_solution(7098103380352573452)
XLA Ops:
  0.0 22.3 %hyena.1 = bf16[32,512]{1,0:T(8,128)(2,1)S(1)} custom-call(bf16[3,32,512]{2,1,0:T(8,128)(2,1)} %proj.1, f32[3,3,32]{2,1,0:T(4,128)} %bitcast.1, bf16[32,512]{1,0:T(8,128)(2,1)} %filt.1, f32[32]{0:T(128)} %gain.1, f32[512,256]{1,0:T(8,128)} %constant.10.clone.w1, f32[256,256]{1,0:T(8,128)} %constant.11.clone.w3, f32[256,256]{1,0:T(8,128)} %constant.12.clone.w4, ...), custom_call_target="tpu_custom_call" | custom-call | flops 200000000 | bytes 2000000 | tf_op jit(solution)/shard_map/hyena/pallas_call | solution.py:386
  22.3 0.6 %copy.11 = bf16[32,512]{1,0:T(8,128)(2,1)} copy(bf16[32,512]{1,0:T(8,128)(2,1)S(1)} %hyena.1) | data formatting | bytes 65536

commit v6 on v5

--- a/solution.py
+++ b/solution.py
@@ -20,9 +20,8 @@
 def tables(blocks, pieces):
     rows = blocks * pieces
     n = rows * LANES
-    order = (np.arange(blocks)[None, :] * pieces + np.arange(pieces)[:, None]).reshape(-1)
     k1 = np.arange(rows) + 0.25
-    first = np.exp(-2j * np.pi * np.outer(k1, order) / rows)
+    first = np.exp(-2j * np.pi * np.outer(k1, np.arange(rows)) / rows)
     turn = np.exp(-2j * np.pi * np.outer(k1, np.arange(LANES)) / n)
     second = np.exp(-2j * np.pi * np.outer(np.arange(LANES), np.arange(LANES)) / LANES)
     back = np.conj(second)
@@ -32,7 +31,7 @@
     w4 = np.block([[back.real, back.imag], [-back.imag, back.real]])
     w6 = np.concatenate([last.real, -last.imag], 1)
     tw = np.stack([turn.real, turn.imag])
-    return tuple(x.astype(np.float32) for x in (w1, w3, w4, w6, tw))
+    return tuple(x.astype(np.float32) for x in (w1, w6, tw, w3, w4))
 
 
 def dot(a, b):
@@ -40,16 +39,16 @@
 
 
 def kernel(
-    blocks, proj, weight, filt, gain, w1, w3, w4, w6, tw, out,
-    proj_v, filt_v, weight_v, gain_s, w1_v, w3_v, w4_v, w6_v, tw_v,
-    halo, taps_v, query_v, filt_s, mix_s, filt_m, mix_m, edge_m, filt_in, mix_in, edge_in, filt_o, mix_o, edge_o, spec_h,
-    w1_b, w3_b, w4_b, w6_b,
-    result, reply_v, back, back_f,
-    load_sem, const_sem, ready, halo_send, halo_recv, filt_send, filt_recv, mix_send, mix_recv, edge_send, edge_recv, send2_sem, recv2_sem,
+    blocks, proj, weight, filt, gain, w1, w6, tw, w3, w4, w1_half, w6_half, tw_half, out,
+    proj_v, filt_v, weight_v, gain_s, w1_v, w6_v, tw_v, w3_v, w4_v, w1_half_v, w6_half_v, tw_half_v,
+    w1_b, w6_b, w3_b, w4_b, w1_half_b, w6_half_b,
+    halo, taps_v, query_v, filt_s, mix_s, filt_m, mix_m, edge_m, filt_in, mix_in, edge_in, edge_o, heads, spec_h,
+    reply_v, back, back_f,
+    load_sem, const_sem, ready, halo_send, halo_recv, filt_send, filt_recv, mix_send, mix_recv, edge_send, edge_recv,
+    send2_sem, recv2_sem,
 ):
     chans = proj.shape[1]
     pieces = proj.shape[2] // LANES
-    rows = blocks * pieces
     me = lax.axis_index("seq")
     groups = blocks // ROW
     homes = groups * 2 * COUNT
@@ -76,7 +75,10 @@
         load.start()
     consts = [
         pltpu.make_async_copy(src, dst, const_sem.at[i])
-        for i, (src, dst) in enumerate([(w1, w1_v), (w3, w3_v), (w4, w4_v), (w6, w6_v), (tw, tw_v)])
+        for i, (src, dst) in enumerate(
+            [(w1, w1_v), (w6, w6_v), (tw, tw_v), (w3, w3_v), (w4, w4_v)]
+            + [(w1_half, w1_half_v), (w6_half, w6_half_v), (tw_half, tw_half_v)]
+        )
     ]
 
     barrier = pltpu.get_barrier_semaphore()
@@ -122,28 +124,33 @@
         pl.semaphore_signal(ready, inc=1, device_id={"seq": me - 1}, device_id_type=MESH)
 
     half = groups // 2
-    turn_of = jnp.where((place < ROW // 2) | (group < half - 1), 0, 1)
-    spans = [[], []]
-    for g in range(groups):
-        spans[0].append(g * ROW)
-        spans[0 if g < half - 1 else 1].append(g * ROW + ROW // 2)
-
-    def send(src, each, dst, send_sem, recv_sem):
+    ahead = half * ROW - ROW // 2
+    counts = (ahead, blocks - ahead)
+    turn_of = jnp.where(me < ahead, 0, 1)
+
+    def send(src, dst, send_sem, recv_sem):
+        step = src.shape[0] // homes
+
         for g in far_first:
             for k in range(2 * COUNT):
                 slot = jnp.where(place >= ROW * 3 // 4, 2 * COUNT - 1 - k, k)
                 h, to = g * (2 * COUNT) + slot, g * ROW + 2 * FIRST + slot
+                part = src.at[pl.ds(h * step, step)]
 
                 @pl.when(to != me)
                 def _():
                     pltpu.make_async_remote_copy(
-                        src_ref=src.at[pl.ds(h * each, each)],
-                        dst_ref=dst.at[pl.ds(me * each, each)],
+                        src_ref=part,
+                        dst_ref=dst.at[:, me],
                         send_sem=send_sem,
                         recv_sem=recv_sem.at[turn_of],
                         device_id={"seq": to},
                         device_id_type=MESH,
                     ).start()
+
+        @pl.when(holder)
+        def _():
+            pltpu.make_async_copy(src.at[pl.ds(mine * step, step)], dst.at[:, me], recv_sem.at[turn_of]).start()
 
     lane = lax.broadcasted_iota(jnp.int32, (blocks, LANES), 1)
 
@@ -165,7 +172,7 @@
     for r in range(pieces):
         filt_s[pl.ds(r, chans, stride=pieces), :] = filt_v[:, tile(r)].astype(f32)
     filt_m[...] = filt_s[...].reshape(chans, pieces, LANES).astype(bf16)
-    send(filt_m, each, filt_in, filt_send, filt_recv)
+    send(filt_m, filt_in, filt_send, filt_recv)
 
     loads[2].wait()
     here = lane[:chans]
@@ -174,8 +181,8 @@
         head, tail = proj_v[j, :, tile(0)].astype(f32), proj_v[j, :, tile(pieces - 1)].astype(f32)
         ends.append(jnp.where(here < LANES // 2, head, tail))
     ends = jnp.where((here >= 6) & (here < 10), pltpu.roll(ends[1], 8, 1), ends[0])
-    edge_m[...] = ends.reshape(homes, each, LANES).astype(bf16)
-    send(edge_m, 1, edge_in, edge_send, edge_recv)
+    edge_m[...] = ends.reshape(edge_m.shape).astype(bf16)
+    send(edge_m, edge_in, edge_send, edge_recv)
 
     for r in range(pieces):
         conv = []
@@ -185,7 +192,7 @@
             conv.append(short(now, before, taps[j]))
         mix_s[pl.ds(r, chans, stride=pieces), :] = conv[0] * conv[1]
     mix_m[...] = mix_s[...].reshape(chans, pieces, LANES).astype(bf16)
-    send(mix_m, each, mix_in, mix_send, mix_recv)
+    send(mix_m, mix_in, mix_send, mix_recv)
 
     edge = pltpu.make_async_remote_copy(
         src_ref=proj_v.at[0, :, pl.ds((pieces - 1) * LANES, LANES)],
@@ -221,59 +228,59 @@
     def _():
         for const in consts:
             const.wait()
-        for src, dst in zip((w1_v, w3_v, w4_v, w6_v), (w1_b, w3_b, w4_b, w6_b)):
+        for src, dst in (
+            (w1_v, w1_b), (w6_v, w6_b), (w3_v, w3_b), (w4_v, w4_b), (w1_half_v, w1_half_b), (w6_half_v, w6_half_b)
+        ):
             dst[...] = src[...].astype(bf16)
-        tr, ti = tw_v[0], tw_v[1]
-        for opened in (filt_o, mix_o, edge_o):
-            opened[...] = jnp.zeros_like(opened)
-        for src, dst in ((filt_m, filt_in), (mix_m, mix_in)):
-            dst[pl.ds(me * each, each)] = src[pl.ds(mine * each, each)]
-        edge_in[me] = edge_m[mine]
+        edge_o[...] = jnp.zeros_like(edge_o)
         chan_lane = lax.broadcasted_iota(jnp.int32, weight_v.shape[1:], 1)
-        row = lax.broadcasted_iota(jnp.int32, (blocks, LANES), 0)
         held = []
         for e in range(each):
             here = chan_lane == mine * each + e
             rows_j = [jnp.sum(jnp.where(here, weight_v[j], 0.0), axis=1, keepdims=True) for j in (1, 2)]
             held.append([[x[i : i + 1, :] for i in range(3)] for x in rows_j])
 
-        def forward(signals):
-            step = dot(w1_b[...], jnp.concatenate(signals, 1))
-            turned = []
+        def arrived(turn, dst, sem):
+            some = dst.at[:, pl.ds(0, counts[turn])]
+            pltpu.make_async_copy(some, some, sem.at[turn]).wait()
+
+        for turn in range(2):
+            count = (half * ROW, blocks)[turn]
+            known = (ahead, blocks)[turn]
+            rows = count * pieces
+            first, last, turns = ((w1_half_b, w6_half_b, tw_half_v), (w1_b, w6_b, tw_v))[turn]
+            tr, ti = turns[0], turns[1]
+            row = lax.broadcasted_iota(jnp.int32, (rows, LANES), 0)
+            column = lax.broadcasted_iota(jnp.int32, (rows, LANES), 1)
+
+            def signal(src, e):
+                got = src[e, :known].astype(f32).reshape(known * pieces, LANES)
+                if known < count:
+                    got = jnp.concatenate([got, jnp.zeros((rows - known * pieces, LANES), f32)], 0)
+                return got
+
+            def forward(signals):
+                step = dot(first[...], jnp.concatenate(signals, 1))
+                turned = []
+                for e in range(each):
+                    re, im = step[:rows, tile(e)], step[rows:, tile(e)]
+                    turned.append(jnp.concatenate([re * tr - im * ti, re * ti + im * tr], 1).astype(bf16))
+                return dot(jnp.concatenate(turned, 0), w3_b[...])
+
+            arrived(turn, filt_in, filt_recv)
+            spec_h[: each * rows] = forward([signal(filt_in, e).astype(bf16) for e in range(each)])
+            arrived(turn, edge_in, edge_recv)
+            fresh = edge_in[0, :known, 0].astype(f32)
+            edge_o[: known * each, :] = fresh.reshape(known * each, LANES)
             for e in range(each):
-                re, im = step[:rows, tile(e)], step[rows:, tile(e)]
-                turned.append(jnp.concatenate([re * tr - im * ti, re * ti + im * tr], 1).astype(bf16))
-            return dot(jnp.concatenate(turned, 0), w3_b[...])
-
-        def take(turn, src, step, lines, dst, sem):
-            count = len(spans[turn]) * (ROW // 2) - (1 if turn == 0 else 0)
-            others = src.at[pl.ds(0, count * step)]
-            pltpu.make_async_copy(others, others, sem.at[turn]).wait()
-            for a in spans[turn]:
-                b = a + ROW // 2
-                fresh = src[a * step : b * step].astype(f32)
-                dst[a * lines : b * lines, :] = fresh.reshape((b - a) * lines, LANES)
-
-        def rows_of(opened, e):
-            return [opened[pl.ds(e * pieces + r, blocks, stride=each * pieces), :] for r in range(pieces)]
-
-        for turn in range(2):
-            take(turn, filt_in, each, each * pieces, filt_o, filt_recv)
-            spec_h[...] = forward([jnp.concatenate(rows_of(filt_o, e), 0).astype(bf16) for e in range(each)])
-            take(turn, edge_in, 1, each, edge_o, edge_recv)
-            heads = []
-            for e in range(each):
-                ends = edge_o[pl.ds(e, blocks, stride=each), :]
+                ends = edge_o[pl.ds(e, count, stride=each), :]
                 conv = []
                 for now, taps in zip((ends, pltpu.roll(ends, LANES - 8, 1)), held[e]):
-                    conv.append(short(now, jnp.where(row == 0, 0.0, pltpu.roll(now, 1, 0)), taps))
-                heads.append((conv[0] * conv[1]).astype(bf16).astype(f32))
-            take(turn, mix_in, each, each * pieces, mix_o, mix_recv)
-            mixes = []
-            for e in range(each):
-                part = rows_of(mix_o, e)
-                part[0] = jnp.where(lane < 2, heads[e], part[0])
-                mixes.append(jnp.concatenate(part, 0).astype(bf16))
+                    conv.append(short(now, jnp.where(row[:count] == 0, 0.0, pltpu.roll(now, 1, 0)), taps))
+                heads[e, pl.ds(0, count, stride=pieces), :] = conv[0] * conv[1]
+            arrived(turn, mix_in, mix_recv)
+            start = (column < 2) & (lax.rem(row, pieces) == 0)
+            mixes = [jnp.where(start, heads[e, :rows], signal(mix_in, e)).astype(bf16) for e in range(each)]
             spec = forward(mixes)
             prods = []
             for e in range(each):
@@ -286,18 +293,14 @@
                 part = inv[e * rows : (e + 1) * rows]
                 re, im = part[:, :LANES], part[:, LANES:]
                 untwist.append(jnp.concatenate([re * tr + im * ti, im * tr - re * ti], 0).astype(bf16))
-            long_out = dot(w6_b[...], jnp.concatenate(untwist, 1))
+            long_out = dot(last[...], jnp.concatenate(untwist, 1))
             for e in range(each):
                 total = long_out[:, tile(e)] + gain_s[mine * each + e] * mixes[e].astype(f32)
-                for r in range(pieces):
-                    result[pl.ds(e * pieces + r, blocks, stride=each * pieces), :] = total[
-                        r * blocks : (r + 1) * blocks
-                    ]
-            reply_v[turn] = result[...].reshape(blocks, each, pieces, LANES).astype(bf16)
+                reply_v[turn, e, :count] = total.reshape(count, pieces, LANES).astype(bf16)
 
             @pl.when((group < half) if turn == 0 else (group >= half))
             def _():
-                back[pl.ds(mine * each, each)] = reply_v[turn, me]
+                back[pl.ds(mine * each, each)] = reply_v[turn, :, me]
 
             early = [(p, g) for p in range(ROW // 2) for g in range(groups) if (g < half) == (turn == 0)]
             late = [(p, g) for p in range(ROW // 2, ROW) for g in range(groups) if turn == 1]
@@ -307,7 +310,7 @@
                 @pl.when(me != a)
                 def _():
                     pltpu.make_async_remote_copy(
-                        src_ref=reply_v.at[turn, a],
+                        src_ref=reply_v.at[turn, :, a],
                         dst_ref=back.at[pl.ds(mine * each, each)],
                         send_sem=send2_sem,
                         recv_sem=recv2_sem,
@@ -331,19 +334,19 @@
     def _():
         edge.wait_send()
 
-    sends = ((filt_m, each, filt_send), (mix_m, each, mix_send), (edge_m, 1, edge_send))
+    sends = ((filt_m, filt_send), (mix_m, mix_send), (edge_m, edge_send))
 
     @pl.when(holder)
     def _():
-        for src, step, sem in sends:
-            sent = src.at[pl.ds(0, (homes - 1) * step)]
+        for src, sem in sends:
+            sent = src.at[pl.ds(0, src.shape[0] // homes * (homes - 1))]
             pltpu.make_async_copy(sent, sent, sem).wait()
-        sent = reply_v.at[0, pl.ds(0, blocks - 1)]
+        sent = reply_v.at[0, :, pl.ds(0, blocks - 1)]
         pltpu.make_async_copy(sent, sent, send2_sem).wait()
 
     @pl.when(jnp.logical_not(holder))
     def _():
-        for src, _, sem in sends:
+        for src, sem in sends:
             pltpu.make_async_copy(src, src, sem).wait()
 
 
@@ -352,7 +355,7 @@
     pieces = tokens // LANES
     each = chans // (blocks // ROW * 2 * COUNT)
     rows = blocks * pieces
-    consts = [jnp.asarray(x) for x in tables(blocks, pieces)]
+    consts = [jnp.asarray(x) for x in tables(blocks, pieces) + tables(blocks // 2, pieces)[:3]]
     weight = jnp.transpose(short_weight, (0, 2, 1))
     dma = pltpu.SemaphoreType.DMA
     scratch = [
@@ -361,6 +364,7 @@
         pltpu.VMEM(weight.shape, f32),
         pltpu.SMEM(skip_gain.shape, f32),
         *[pltpu.VMEM(x.shape, x.dtype) for x in consts],
+        *[pltpu.VMEM(consts[i].shape, bf16) for i in (0, 1, 3, 4, 5, 6)],
         pltpu.VMEM((chans, LANES), bf16),
         pltpu.VMEM((16, LANES), f32),
         pltpu.VMEM((chans, tokens), f32),
@@ -368,25 +372,22 @@
         pltpu.VMEM((chans * pieces, LANES), f32),
         pltpu.VMEM((chans, pieces, LANES), bf16),
         pltpu.VMEM((chans, pieces, LANES), bf16),
-        pltpu.VMEM((chans // each, each, LANES), bf16),
-        pltpu.VMEM((blocks * each, pieces, LANES), bf16),
-        pltpu.VMEM((blocks * each, pieces, LANES), bf16),
-        pltpu.VMEM((blocks, each, LANES), bf16),
-        pltpu.VMEM((blocks * each * pieces, LANES), f32),
-        pltpu.VMEM((blocks * each * pieces, LANES), f32),
+        pltpu.VMEM((chans // each, 1, each, LANES), bf16),
+        pltpu.VMEM((each, blocks, pieces, LANES), bf16),
+        pltpu.VMEM((each, blocks, pieces, LANES), bf16),
+        pltpu.VMEM((1, blocks, 1, each, LANES), bf16),
         pltpu.VMEM((blocks * each, LANES), f32),
+        pltpu.VMEM((each, rows, LANES), f32),
         pltpu.VMEM((each * rows, 2 * LANES), f32),
-        *[pltpu.VMEM(x.shape, bf16) for x in consts[:4]],
-        pltpu.VMEM((rows * each, LANES), f32),
-        pltpu.VMEM((2, blocks, each, pieces, LANES), bf16),
+        pltpu.VMEM((2, each, blocks, pieces, LANES), bf16),
         pltpu.VMEM((chans, pieces, LANES), bf16),
         pltpu.VMEM((chans * pieces, LANES), f32),
-        dma((4,)), dma((5,)), pltpu.SemaphoreType.REGULAR, dma, dma, *[dma, dma((2,))] * 3, dma, dma,
+        dma((4,)), dma((8,)), pltpu.SemaphoreType.REGULAR, dma, dma, *[dma, dma((2,))] * 3, dma, dma,
     ]
     return pl.pallas_call(
         functools.partial(kernel, blocks),
         out_shape=pltpu.VMEM((chans, tokens), bf16),
-        in_specs=[pl.BlockSpec(memory_space=pl.ANY)] * 9,
+        in_specs=[pl.BlockSpec(memory_space=pl.ANY)] * 12,
         out_specs=pl.BlockSpec(memory_space=pltpu.VMEM),
         scratch_shapes=scratch,
         compiler_params=pltpu.CompilerParams(

time: 23.1 us -> 22.4 us (0.970)
  Pallas kernels: 22.3 us -> 21.7 us
    pallas_call x1, Pallas kernels: 22.3 us -> 21.7 us  [shards(): pl.pallas_call(functools.partial(kernel, blocks), out_shape=pltpu.VMEM((c...]
where the time goes in v6:
time: 22.4 us; the launch traced here: 22.3 us
  Pallas kernels  21.7 us (97%)
  local copies, waits for them, and re-layouts  0.62 us (3%)
    pallas_call x1, Pallas kernels, shards(): pl.pallas_call(functools.partial(kernel, blocks), out_shape=pltpu.VMEM((c...  21.7 us
    unnamed x1, local copies, waits for them, and re-layouts  0.62 us

profile of v6, /device:TPU:1, one launch (start us, length us, event | category | flops | bytes accessed | tf_op | source)
XLA Modules:
  0.0 22.3 jit_solution(839963821116246416)
XLA Ops:
  0.0 21.7 %hyena.1 = bf16[32,512]{1,0:T(8,128)(2,1)S(1)} custom-call(bf16[3,32,512]{2,1,0:T(8,128)(2,1)} %proj.1, f32[3,3,32]{2,1,0:T(4,128)} %bitcast.1, bf16[32,512]{1,0:T(8,128)(2,1)} %filt.1, f32[32]{0:T(128)} %gain.1, f32[512,256]{1,0:T(8,128)} %constant.16.clone.w1, f32[256,512]{1,0:T(8,128)} %constant.17.clone.w6, f32[2,256,128]{2,1,0:T(8,128)} %constant.18.clone.tw, ...), custom_call_target="tpu_custom_call" | custom-call | flops 200000000 | bytes 2000000 | tf_op jit(solution)/shard_map/hyena/pallas_call | solution.py:387
  21.7 0.6 %copy.14 = bf16[32,512]{1,0:T(8,128)(2,1)} copy(bf16[32,512]{1,0:T(8,128)(2,1)S(1)} %hyena.1) | data formatting | bytes 65536

commit v7 on v6

--- a/solution.py
+++ b/solution.py
@@ -12,7 +12,7 @@
 LANES = 128
 ROW = 16
 FIRST, COUNT = 1, 1
-GREET = (5, 6, 4, 7, 3, 0, 2, 1)
+GREET = (0, 2, 3, 1, 4, 5, 6, 7)
 f32 = jnp.float32
 bf16 = jnp.bfloat16
 
@@ -69,7 +69,10 @@
 
     loads = [
         pltpu.make_async_copy(src, dst, load_sem.at[i])
-        for i, (src, dst) in enumerate([(weight, weight_v), (filt, filt_v), (proj, proj_v), (gain, gain_s)])
+        for i, (src, dst) in enumerate(
+            [(weight, weight_v), (filt, filt_v), (proj.at[1], proj_v.at[1]), (proj.at[2], proj_v.at[2])]
+            + [(proj.at[0], proj_v.at[0]), (gain, gain_s)]
+        )
     ]
     for load in loads:
         load.start()
@@ -124,9 +127,10 @@
         pl.semaphore_signal(ready, inc=1, device_id={"seq": me - 1}, device_id_type=MESH)
 
     half = groups // 2
-    ahead = half * ROW - ROW // 2
-    counts = (ahead, blocks - ahead)
-    turn_of = jnp.where(me < ahead, 0, 1)
+    ends_at = (ROW // 2, half * ROW - ROW // 2, blocks)
+    counts = [b - a for a, b in zip((0, *ends_at), ends_at)]
+    turn_of = sum((me >= b).astype(jnp.int32) for b in ends_at[:-1])
+    asked = [range(1), range(1, half), range(half, groups)]
 
     def send(src, dst, send_sem, recv_sem):
         step = src.shape[0] // homes
@@ -175,6 +179,7 @@
     send(filt_m, filt_in, filt_send, filt_recv)
 
     loads[2].wait()
+    loads[3].wait()
     here = lane[:chans]
     ends = []
     for j in (1, 2):
@@ -194,6 +199,7 @@
     mix_m[...] = mix_s[...].reshape(chans, pieces, LANES).astype(bf16)
     send(mix_m, mix_in, mix_send, mix_recv)
 
+    loads[4].wait()
     edge = pltpu.make_async_remote_copy(
         src_ref=proj_v.at[0, :, pl.ds((pieces - 1) * LANES, LANES)],
         dst_ref=halo,
@@ -222,7 +228,7 @@
         before = (halo[...] if r == 0 else proj_v[0, :, tile(r - 1)]).astype(f32)
         query_v[:, tile(r)] = short(now, before, taps[0])
 
-    loads[3].wait()
+    loads[5].wait()
 
     @pl.when(holder)
     def _():
@@ -244,11 +250,25 @@
             some = dst.at[:, pl.ds(0, counts[turn])]
             pltpu.make_async_copy(some, some, sem.at[turn]).wait()
 
-        for turn in range(2):
-            count = (half * ROW, blocks)[turn]
-            known = (ahead, blocks)[turn]
+        def answer(places):
+            for turn, place_to, g in places:
+                a = g * ROW + place_to
+
+                @pl.when(me != a)
+                def _():
+                    pltpu.make_async_remote_copy(
+                        src_ref=reply_v.at[turn, :, a],
+                        dst_ref=back.at[pl.ds(mine * each, each)],
+                        send_sem=send2_sem,
+                        recv_sem=recv2_sem,
+                        device_id={"seq": a},
+                        device_id_type=MESH,
+                    ).start()
+
+        for turn, known in enumerate(ends_at):
+            count = half * ROW if turn < 2 else blocks
             rows = count * pieces
-            first, last, turns = ((w1_half_b, w6_half_b, tw_half_v), (w1_b, w6_b, tw_v))[turn]
+            first, last, turns = (w1_half_b, w6_half_b, tw_half_v) if turn < 2 else (w1_b, w6_b, tw_v)
             tr, ti = turns[0], turns[1]
             row = lax.broadcasted_iota(jnp.int32, (rows, LANES), 0)
             column = lax.broadcasted_iota(jnp.int32, (rows, LANES), 1)
@@ -293,30 +313,31 @@
                 part = inv[e * rows : (e + 1) * rows]
                 re, im = part[:, :LANES], part[:, LANES:]
                 untwist.append(jnp.concatenate([re * tr + im * ti, im * tr - re * ti], 0).astype(bf16))
-            long_out = dot(last[...], jnp.concatenate(untwist, 1))
-            for e in range(each):
-                total = long_out[:, tile(e)] + gain_s[mine * each + e] * mixes[e].astype(f32)
-                reply_v[turn, e, :count] = total.reshape(count, pieces, LANES).astype(bf16)
-
-            @pl.when((group < half) if turn == 0 else (group >= half))
+            untwisted = jnp.concatenate(untwist, 1)
+
+            def finish(firsts):
+                some = [slice(a * pieces, (a + ROW // 2) * pieces) for a in firsts]
+                long_out = dot(jnp.concatenate([last[x] for x in some], 0), untwisted)
+                for e in range(each):
+                    mixed = jnp.concatenate([mixes[e][x] for x in some], 0).astype(f32)
+                    total = long_out[:, tile(e)] + gain_s[mine * each + e] * mixed
+                    total = total.reshape(len(some) * (ROW // 2), pieces, LANES).astype(bf16)
+                    for i, a in enumerate(firsts):
+                        reply_v[turn, e, a : a + ROW // 2] = total[i * (ROW // 2) : (i + 1) * (ROW // 2)]
+
+            near, far, late = range(ROW // 4), range(ROW // 4, ROW // 2), range(ROW // 2, ROW)
+            finish([g * ROW for g in asked[turn]])
+            answer([(turn, p, g) for p in near for g in asked[turn]])
+            if turn == 0:
+                answer([(0, p, g) for p in far for g in asked[0]])
+            if turn == 2:
+                answer([(t, p, g) for p in far for t in (1, 2) for g in asked[t]])
+                finish([g * ROW + ROW // 2 for g in range(groups)])
+                answer([(2, p, g) for p in late for g in range(groups)])
+
+            @pl.when((group >= asked[turn].start) & (group < asked[turn].stop))
             def _():
                 back[pl.ds(mine * each, each)] = reply_v[turn, :, me]
-
-            early = [(p, g) for p in range(ROW // 2) for g in range(groups) if (g < half) == (turn == 0)]
-            late = [(p, g) for p in range(ROW // 2, ROW) for g in range(groups) if turn == 1]
-            for place_to, g in early + late:
-                a = g * ROW + place_to
-
-                @pl.when(me != a)
-                def _():
-                    pltpu.make_async_remote_copy(
-                        src_ref=reply_v.at[turn, :, a],
-                        dst_ref=back.at[pl.ds(mine * each, each)],
-                        send_sem=send2_sem,
-                        recv_sem=recv2_sem,
-                        device_id={"seq": a},
-                        device_id_type=MESH,
-                    ).start()
 
         others = back.at[pl.ds(0, chans - each)]
         pltpu.make_async_copy(others, others, recv2_sem).wait()
@@ -379,10 +400,10 @@
         pltpu.VMEM((blocks * each, LANES), f32),
         pltpu.VMEM((each, rows, LANES), f32),
         pltpu.VMEM((each * rows, 2 * LANES), f32),
-        pltpu.VMEM((2, each, blocks, pieces, LANES), bf16),
+        pltpu.VMEM((3, each, blocks, pieces, LANES), bf16),
         pltpu.VMEM((chans, pieces, LANES), bf16),
         pltpu.VMEM((chans * pieces, LANES), f32),
-        dma((4,)), dma((8,)), pltpu.SemaphoreType.REGULAR, dma, dma, *[dma, dma((2,))] * 3, dma, dma,
+        dma((6,)), dma((8,)), pltpu.SemaphoreType.REGULAR, dma, dma, *[dma, dma((3,))] * 3, dma, dma,
     ]
     return pl.pallas_call(
         functools.partial(kernel, blocks),

time: 22.4 us -> 22.2 us (level)
  the two profiles are of different devices: /device:TPU:1 before, /device:TPU:7 now
where the time goes in v7:
time: 22.2 us; the launch traced here: 22 us
  Pallas kernels  21.4 us (96%)
  local copies, waits for them, and re-layouts  0.62 us (3%)
    pallas_call x1, Pallas kernels, shards(): pl.pallas_call(functools.partial(kernel, blocks), out_shape=pltpu.VMEM((c...  21.4 us
    unnamed x1, local copies, waits for them, and re-layouts  0.62 us

profile of v7, /device:TPU:7, one launch (start us, length us, event | category | flops | bytes accessed | tf_op | source)
XLA Modules:
  0.0 22.0 jit_solution(10073112585798558814)
XLA Ops:
  0.0 21.4 %hyena.1 = bf16[32,512]{1,0:T(8,128)(2,1)S(1)} custom-call(bf16[3,32,512]{2,1,0:T(8,128)(2,1)} %proj.1, f32[3,3,32]{2,1,0:T(4,128)} %bitcast.1, bf16[32,512]{1,0:T(8,128)(2,1)} %filt.1, f32[32]{0:T(128)} %gain.1, f32[512,256]{1,0:T(8,128)} %constant.16.clone.w1, f32[256,512]{1,0:T(8,128)} %constant.17.clone.w6, f32[2,256,128]{2,1,0:T(8,128)} %constant.18.clone.tw, ...), custom_call_target="tpu_custom_call" | custom-call | flops 200000000 | bytes 2000000 | tf_op jit(solution)/shard_map/hyena/pallas_call | solution.py:408
  21.4 0.6 %copy.14 = bf16[32,512]{1,0:T(8,128)(2,1)} copy(bf16[32,512]{1,0:T(8,128)(2,1)S(1)} %hyena.1) | data formatting | bytes 65536

commit v8 on v7

--- a/solution.py
+++ b/solution.py
@@ -42,9 +42,9 @@
     blocks, proj, weight, filt, gain, w1, w6, tw, w3, w4, w1_half, w6_half, tw_half, out,
     proj_v, filt_v, weight_v, gain_s, w1_v, w6_v, tw_v, w3_v, w4_v, w1_half_v, w6_half_v, tw_half_v,
     w1_b, w6_b, w3_b, w4_b, w1_half_b, w6_half_b,
-    halo, taps_v, query_v, filt_s, mix_s, filt_m, mix_m, edge_m, filt_in, mix_in, edge_in, edge_o, heads, spec_h,
+    halo, taps_v, query_v, filt_s, mix_s, filt_m, mix_m, filt_in, mix_in, edge_o, heads, spec_h,
     reply_v, back, back_f,
-    load_sem, const_sem, ready, halo_send, halo_recv, filt_send, filt_recv, mix_send, mix_recv, edge_send, edge_recv,
+    load_sem, const_sem, ready, halo_send, halo_recv, filt_send, filt_recv, mix_send, mix_recv,
     send2_sem, recv2_sem,
 ):
     chans = proj.shape[1]
@@ -172,12 +172,6 @@
     taps_t = taps_v[...].T[:chans]
     taps = [[taps_t[:, 3 * j + i : 3 * j + i + 1] for i in range(3)] for j in range(3)]
 
-    loads[1].wait()
-    for r in range(pieces):
-        filt_s[pl.ds(r, chans, stride=pieces), :] = filt_v[:, tile(r)].astype(f32)
-    filt_m[...] = filt_s[...].reshape(chans, pieces, LANES).astype(bf16)
-    send(filt_m, filt_in, filt_send, filt_recv)
-
     loads[2].wait()
     loads[3].wait()
     here = lane[:chans]
@@ -186,8 +180,14 @@
         head, tail = proj_v[j, :, tile(0)].astype(f32), proj_v[j, :, tile(pieces - 1)].astype(f32)
         ends.append(jnp.where(here < LANES // 2, head, tail))
     ends = jnp.where((here >= 6) & (here < 10), pltpu.roll(ends[1], 8, 1), ends[0])
-    edge_m[...] = ends.reshape(edge_m.shape).astype(bf16)
-    send(edge_m, edge_in, edge_send, edge_recv)
+
+    loads[1].wait()
+    for r in range(pieces):
+        filt_s[pl.ds(r, chans, stride=pieces), :] = filt_v[:, tile(r)].astype(f32)
+    parts = [filt_s[...].reshape(homes, each, pieces, LANES), ends.reshape(homes, 1, each, LANES)]
+    filt_m[...] = jnp.concatenate(parts, 1).reshape(filt_m.shape).astype(bf16)
+    send(filt_m, filt_in, filt_send, filt_recv)
+
 
     for r in range(pieces):
         conv = []
@@ -288,9 +288,7 @@
                 return dot(jnp.concatenate(turned, 0), w3_b[...])
 
             arrived(turn, filt_in, filt_recv)
-            spec_h[: each * rows] = forward([signal(filt_in, e).astype(bf16) for e in range(each)])
-            arrived(turn, edge_in, edge_recv)
-            fresh = edge_in[0, :known, 0].astype(f32)
+            fresh = filt_in[each, :known].astype(f32)
             edge_o[: known * each, :] = fresh.reshape(known * each, LANES)
             for e in range(each):
                 ends = edge_o[pl.ds(e, count, stride=each), :]
@@ -298,6 +296,7 @@
                 for now, taps in zip((ends, pltpu.roll(ends, LANES - 8, 1)), held[e]):
                     conv.append(short(now, jnp.where(row[:count] == 0, 0.0, pltpu.roll(now, 1, 0)), taps))
                 heads[e, pl.ds(0, count, stride=pieces), :] = conv[0] * conv[1]
+            spec_h[: each * rows] = forward([signal(filt_in, e).astype(bf16) for e in range(each)])
             arrived(turn, mix_in, mix_recv)
             start = (column < 2) & (lax.rem(row, pieces) == 0)
             mixes = [jnp.where(start, heads[e, :rows], signal(mix_in, e)).astype(bf16) for e in range(each)]
@@ -355,7 +354,7 @@
     def _():
         edge.wait_send()
 
-    sends = ((filt_m, filt_send), (mix_m, mix_send), (edge_m, edge_send))
+    sends = ((filt_m, filt_send), (mix_m, mix_send))
 
     @pl.when(holder)
     def _():
@@ -391,19 +390,17 @@
         pltpu.VMEM((chans, tokens), f32),
         pltpu.VMEM((chans * pieces, LANES), f32),
         pltpu.VMEM((chans * pieces, LANES), f32),
+        pltpu.VMEM((chans // each * (each + 1), pieces, LANES), bf16),
         pltpu.VMEM((chans, pieces, LANES), bf16),
-        pltpu.VMEM((chans, pieces, LANES), bf16),
-        pltpu.VMEM((chans // each, 1, each, LANES), bf16),
+        pltpu.VMEM((each + 1, blocks, pieces, LANES), bf16),
         pltpu.VMEM((each, blocks, pieces, LANES), bf16),
-        pltpu.VMEM((each, blocks, pieces, LANES), bf16),
-        pltpu.VMEM((1, blocks, 1, each, LANES), bf16),
         pltpu.VMEM((blocks * each, LANES), f32),
         pltpu.VMEM((each, rows, LANES), f32),
         pltpu.VMEM((each * rows, 2 * LANES), f32),
         pltpu.VMEM((3, each, blocks, pieces, LANES), bf16),
         pltpu.VMEM((chans, pieces, LANES), bf16),
         pltpu.VMEM((chans * pieces, LANES), f32),
-        dma((6,)), dma((8,)), pltpu.SemaphoreType.REGULAR, dma, dma, *[dma, dma((3,))] * 3, dma, dma,
+        dma((6,)), dma((8,)), pltpu.SemaphoreType.REGULAR, dma, dma, *[dma, dma((3,))] * 2, dma, dma,
     ]
     return pl.pallas_call(
         functools.partial(kernel, blocks),

time: 22.2 us -> 22.1 us (level)
  no operation moved by 1% of the time
where the time goes in v8:
time: 22.1 us; the launch traced here: 21.9 us
  Pallas kernels  21.3 us (96%)
  local copies, waits for them, and re-layouts  0.62 us (3%)
    pallas_call x1, Pallas kernels, shards(): pl.pallas_call(functools.partial(kernel, blocks), out_shape=pltpu.VMEM((c...  21.3 us
    unnamed x1, local copies, waits for them, and re-layouts  0.62 us

profile of v8, /device:TPU:7, one launch (start us, length us, event | category | flops | bytes accessed | tf_op | source)
XLA Modules:
  0.0 21.9 jit_solution(10821776794594018876)
XLA Ops:
  0.0 21.3 %hyena.1 = bf16[32,512]{1,0:T(8,128)(2,1)S(1)} custom-call(bf16[3,32,512]{2,1,0:T(8,128)(2,1)} %proj.1, f32[3,3,32]{2,1,0:T(4,128)} %bitcast.1, bf16[32,512]{1,0:T(8,128)(2,1)} %filt.1, f32[32]{0:T(128)} %gain.1, f32[512,256]{1,0:T(8,128)} %constant.16.clone.w1, f32[256,512]{1,0:T(8,128)} %constant.17.clone.w6, f32[2,256,128]{2,1,0:T(8,128)} %constant.18.clone.tw, ...), custom_call_target="tpu_custom_call" | custom-call | flops 200000000 | bytes 2000000 | tf_op jit(solution)/shard_map/hyena/pallas_call | solution.py:405
  21.3 0.6 %copy.14 = bf16[32,512]{1,0:T(8,128)(2,1)} copy(bf16[32,512]{1,0:T(8,128)(2,1)S(1)} %hyena.1) | data formatting | bytes 65536

commit v9 on v8

--- a/solution.py
+++ b/solution.py
@@ -279,10 +279,11 @@
                     got = jnp.concatenate([got, jnp.zeros((rows - known * pieces, LANES), f32)], 0)
                 return got
 
-            def forward(signals):
-                step = dot(first[...], jnp.concatenate(signals, 1))
+            def forward(signals, step=None):
+                if step is None:
+                    step = dot(first[...], jnp.concatenate(signals, 1))
                 turned = []
-                for e in range(each):
+                for e in range(len(signals)):
                     re, im = step[:rows, tile(e)], step[rows:, tile(e)]
                     turned.append(jnp.concatenate([re * tr - im * ti, re * ti + im * tr], 1).astype(bf16))
                 return dot(jnp.concatenate(turned, 0), w3_b[...])
@@ -300,13 +301,17 @@
             arrived(turn, mix_in, mix_recv)
             start = (column < 2) & (lax.rem(row, pieces) == 0)
             mixes = [jnp.where(start, heads[e, :rows], signal(mix_in, e)).astype(bf16) for e in range(each)]
-            spec = forward(mixes)
+            pairs = [mixes[e : e + 2] for e in range(0, each, 2)]
+            steps = [dot(first[...], jnp.concatenate(pair, 1)) for pair in pairs]
+            spec = jnp.concatenate([forward(pair, step) for pair, step in zip(pairs, steps)], 0)
             prods = []
             for e in range(each):
                 x, h = spec[e * rows : (e + 1) * rows], spec_h[e * rows : (e + 1) * rows]
                 xr, xi, hr, hi = x[:, :LANES], x[:, LANES:], h[:, :LANES], h[:, LANES:]
                 prods.append(jnp.concatenate([xr * hr - xi * hi, xr * hi + xi * hr], 1).astype(bf16))
-            inv = dot(jnp.concatenate(prods, 0), w4_b[...])
+            inv = jnp.concatenate(
+                [dot(jnp.concatenate(prods[e : e + 2], 0), w4_b[...]) for e in range(0, each, 2)], 0
+            )
             untwist = []
             for e in range(each):
                 part = inv[e * rows : (e + 1) * rows]

time: 22.1 us -> 22.1 us (level)
  the two profiles are of different devices: /device:TPU:7 before, /device:TPU:15 now
where the time goes in v9:
time: 22.1 us; the launch traced here: 21.9 us
  Pallas kernels  21.3 us (96%)
  local copies, waits for them, and re-layouts  0.62 us (3%)
    pallas_call x1, Pallas kernels, shards(): pl.pallas_call(functools.partial(kernel, blocks), out_shape=pltpu.VMEM((c...  21.3 us
    unnamed x1, local copies, waits for them, and re-layouts  0.62 us

profile of v9, /device:TPU:15, one launch (start us, length us, event | category | flops | bytes accessed | tf_op | source)
XLA Modules:
  0.0 21.9 jit_solution(5138175254242130701)
XLA Ops:
  0.0 21.3 %hyena.1 = bf16[32,512]{1,0:T(8,128)(2,1)S(1)} custom-call(bf16[3,32,512]{2,1,0:T(8,128)(2,1)} %proj.1, f32[3,3,32]{2,1,0:T(4,128)} %bitcast.1, bf16[32,512]{1,0:T(8,128)(2,1)} %filt.1, f32[32]{0:T(128)} %gain.1, f32[512,256]{1,0:T(8,128)} %constant.16.clone.w1, f32[256,512]{1,0:T(8,128)} %constant.17.clone.w6, f32[2,256,128]{2,1,0:T(8,128)} %constant.18.clone.tw, ...), custom_call_target="tpu_custom_call" | custom-call | flops 200000000 | bytes 2000000 | tf_op jit(solution)/shard_map/hyena/pallas_call | solution.py:410
  21.3 0.6 %copy.14 = bf16[32,512]{1,0:T(8,128)(2,1)} copy(bf16[32,512]{1,0:T(8,128)(2,1)S(1)} %hyena.1) | data formatting | bytes 65536
